TPU v7x, 256 devices: a whole 4x4x8 slice. The times are simulated.
256 devices in a mesh: pipe: 32 (over z_lo, x, core), tensor: 8 (over y, z_hi).
Axes of the slice: x: 4, y: 4, z: 8 (z_hi: 2, z_lo: 4; z = z_hi * 4 + z_lo), core: 2. Of those that a mesh axis runs over, the one named last changes fastest.
Arguments:
- down_prev: bfloat16 [32, 256, 4096], P('pipe', 'tensor'), may hold values from -6 to 6
- up_prev: bfloat16 [32, 256, 4096], P('pipe', 'tensor'), may hold values from -6 to 6
- down_stash: bfloat16 [32, 256, 4096], P('pipe', 'tensor'), may hold values from -6 to 6
- up_stash: bfloat16 [32, 256, 4096], P('pipe', 'tensor'), may hold values from -6 to 6
- down_cot: bfloat16 [32, 256, 4096], P('pipe', 'tensor'), may hold values from -0.75 to 0.75
- up_cot: bfloat16 [32, 256, 4096], P('pipe', 'tensor'), may hold values from -0.75 to 0.75
- boundary: bfloat16 [4, 256, 4096], P(None, 'tensor'), may hold values from -3 to 3
- segment_ids: int32 [4, 32, 256], P(None, 'pipe'), may hold values from 0 to 31, never falling along the last dimension, each value on 1 to 128 neighbouring positions
- value_weight: bfloat16 [32, 2, 4096, 1024], P('pipe', None, None, 'tensor'), as said below
- output_weight: bfloat16 [32, 2, 1024, 4096], P('pipe', None, 'tensor'), as said below
Outputs:
- down_out: bfloat16 [32, 256, 4096], P('pipe', 'tensor')
- up_out: bfloat16 [32, 256, 4096], P('pipe', 'tensor')
- down_back: bfloat16 [32, 256, 4096], P('pipe', 'tensor')
- up_back: bfloat16 [32, 256, 4096], P('pipe', 'tensor')
- value_grad: float32 [32, 4096, 1024], P('pipe', None, 'tensor')
- output_grad: float32 [32, 1024, 4096], P('pipe', 'tensor')
Inputs may be any that keep to these rules, and one draw needn't show every extreme that they name: `segment_ids`: ids never fall along a micro-batch's tokens. `value_weight`: entry [r, 1] equals entry [31 - r, 0]: both copies of a section are equal. `output_weight`: entry [r, 1] equals entry [31 - r, 0]: both copies of a section are equal.
All inputs are finite; a program needn't handle non-finite values.
Results may differ from a plain program's by a relative error of at most 0.012.
Values may be sent and summed in bfloat16 or wider, within the bound.
No kernel may reach another device: no remote copies, remote signals or barrier semaphores. Data moves between devices by JAX's collectives and lax.ppermute only.
A program may use at most 128 MiB of HBM per device.

v0:
```python
import jax
import jax.numpy as jnp
from jax import lax
from jax.sharding import PartitionSpec as P

eps = 1e-05


def passed_along(shard, axis, by):
    devices = lax.axis_size(axis)
    pairs = [(i, i + by) for i in range(devices) if 0 <= i + by < devices]
    return lax.ppermute(shard, axis, pairs)


def segment_mask(segment_row):
    positions = jnp.arange(segment_row.shape[0], dtype=jnp.int32)
    causal = positions[:, None] >= positions[None, :]
    same_segment = segment_row[:, None] == segment_row[None, :]
    allowed = jnp.logical_and(causal, same_segment)
    return (
        allowed.astype(jnp.bfloat16),
        jnp.sum(allowed.astype(jnp.float32), axis=1, keepdims=True),
    )


def normalize(inputs):
    widened = inputs.astype(jnp.float32)
    inverse_rms = lax.rsqrt(jnp.mean(widened * widened, axis=-1, keepdims=True) + eps)
    return (widened * inverse_rms, inverse_rms)


def contract(left_side, right_side, left_dim, right_dim):
    return lax.dot_general(
        left_side,
        right_side,
        (((left_dim,), (right_dim,)), ((), ())),
        preferred_element_type=jnp.float32,
    )


def tensor_sum(partial_term):
    return lax.psum_scatter(
        partial_term.astype(jnp.bfloat16), "tensor", scatter_dimension=0, tiled=True
    ).astype(jnp.float32)


def layer_forward(gathered_in, own_rows, segment_row, value_proj, output_proj):
    allowed, counts = segment_mask(segment_row)
    normed = normalize(gathered_in)[0].astype(jnp.bfloat16)
    values = jnp.dot(normed, value_proj, preferred_element_type=jnp.float32).astype(jnp.bfloat16)
    mixed_values = (jnp.dot(allowed, values, preferred_element_type=jnp.float32) / counts).astype(
        jnp.bfloat16
    )
    summed = tensor_sum(jnp.dot(mixed_values, output_proj, preferred_element_type=jnp.float32))
    return (own_rows.astype(jnp.float32) + summed).astype(jnp.bfloat16)


def layer_backward(
    gathered_in, gathered_grad, own_rows, own_grad, segment_row, value_proj, output_proj
):
    allowed, counts = segment_mask(segment_row)
    normed = normalize(gathered_in)[0].astype(jnp.bfloat16)
    values = jnp.dot(normed, value_proj, preferred_element_type=jnp.float32).astype(jnp.bfloat16)
    mixed_values = (jnp.dot(allowed, values, preferred_element_type=jnp.float32) / counts).astype(
        jnp.bfloat16
    )
    output_grad = contract(mixed_values, gathered_grad, 0, 0)
    scaled = (contract(gathered_grad, output_proj, 1, 1) / counts).astype(jnp.bfloat16)
    value_act = contract(allowed, scaled, 0, 0).astype(jnp.bfloat16)
    value_grad = contract(normed, value_act, 0, 0)
    normed_grad = tensor_sum(contract(value_act, value_proj, 1, 1))
    own_normed, own_inverse = normalize(own_rows)
    project = jnp.mean(normed_grad * own_normed, axis=-1, keepdims=True)
    input_grad = own_grad.astype(jnp.float32) + own_inverse * (normed_grad - own_normed * project)
    return (input_grad.astype(jnp.bfloat16), value_grad, output_grad)


def local(
    down_prev,
    up_prev,
    down_stash,
    up_stash,
    down_cot,
    up_cot,
    boundary,
    segment_ids,
    value_weight,
    output_weight,
):
    pipe_count = lax.axis_size("pipe")
    section_index = lax.axis_index("pipe")
    from_below = passed_along((down_prev[0], up_cot[0]), "pipe", 1)
    from_above = passed_along((up_prev[0], down_cot[0]), "pipe", -1)
    is_first = section_index == 0
    is_last = section_index == pipe_count - 1
    down_input = jnp.where(is_first, boundary[0], from_below[0])
    up_upstream = jnp.where(is_first, boundary[3], from_below[1])
    up_input = jnp.where(is_last, boundary[1], from_above[0])
    down_upstream = jnp.where(is_last, boundary[2], from_above[1])
    gathered = (
        lax.all_gather(down_input, "tensor", axis=0, tiled=True),
        lax.all_gather(up_input, "tensor", axis=0, tiled=True),
        lax.all_gather(down_stash[0], "tensor", axis=0, tiled=True),
        lax.all_gather(up_stash[0], "tensor", axis=0, tiled=True),
        lax.all_gather(down_upstream, "tensor", axis=0, tiled=True),
        lax.all_gather(up_upstream, "tensor", axis=0, tiled=True),
    )
    down_result = layer_forward(
        gathered[0], down_input, segment_ids[0, 0], value_weight[0, 0], output_weight[0, 0]
    )
    up_result = layer_forward(
        gathered[1], up_input, segment_ids[1, 0], value_weight[0, 1], output_weight[0, 1]
    )
    down_input_grad, down_value, down_output = layer_backward(
        gathered[2],
        gathered[4],
        down_stash[0],
        down_upstream,
        segment_ids[2, 0],
        value_weight[0, 0],
        output_weight[0, 0],
    )
    up_input_grad, up_value, up_output = layer_backward(
        gathered[3],
        gathered[5],
        up_stash[0],
        up_upstream,
        segment_ids[3, 0],
        value_weight[0, 1],
        output_weight[0, 1],
    )
    model_width, head_width = up_value.shape
    outgoing = jnp.stack(
        [
            up_value.astype(jnp.bfloat16),
            up_output.astype(jnp.bfloat16).reshape(model_width, head_width),
        ]
    )
    pieces = outgoing.reshape(2, pipe_count, model_width // pipe_count, head_width)
    spread = lax.all_to_all(pieces, "pipe", split_axis=1, concat_axis=1, tiled=True)
    turned = jnp.flip(spread, 1)
    returned = lax.all_to_all(turned, "pipe", split_axis=1, concat_axis=1, tiled=True)
    received = returned.reshape(2, model_width, head_width)
    own_value = lax.optimization_barrier(down_value.astype(jnp.bfloat16)).astype(jnp.float32)
    own_output = lax.optimization_barrier(down_output.astype(jnp.bfloat16)).astype(jnp.float32)
    value_total = own_value + received[0].astype(jnp.float32)
    output_total = own_output + received[1].reshape(down_output.shape).astype(jnp.float32)
    return (
        down_result[None],
        up_result[None],
        down_input_grad[None],
        up_input_grad[None],
        value_total[None],
        output_total[None],
    )


def solution(mesh):
    placed = (
        P("pipe", "tensor", None),
        P("pipe", "tensor", None),
        P("pipe", "tensor", None),
        P("pipe", "tensor", None),
        P("pipe", "tensor", None),
        P("pipe", "tensor", None),
        P(None, "tensor", None),
        P(None, "pipe", None),
        P("pipe", None, None, "tensor"),
        P("pipe", None, "tensor", None),
    )
    return jax.shard_map(
        local,
        mesh=mesh,
        in_specs=placed,
        out_specs=(
            P("pipe", "tensor", None),
            P("pipe", "tensor", None),
            P("pipe", "tensor", None),
            P("pipe", "tensor", None),
            P("pipe", None, "tensor"),
            P("pipe", "tensor", None),
        ),
        check_vma=False,
    )
```

profile of v0, /device:TPU:1, one launch (start us, length us, event | category | flops | bytes accessed | tf_op | source)
XLA Modules:
  0.0 914.3 jit_solution(3105517746679622277)
XLA Ops:
  7.2 4.5 collective-permute-start
  11.7 1.9 collective-permute-start.1
  13.7 1.9 collective-permute-start.2
  15.6 3.6 collective-permute-start.3
  19.3 0.3 collective-permute-done.1
  19.6 2.8 collective-permute-done.2
  22.4 0.4 collective-permute-done.3
  22.9 2.2 bitcast_select_fusion
  25.1 0.7 all-gather.13.cloned.1.call-update
  25.9 0.7 all-gather.11.cloned.1.call-update
  26.6 0.5 all-gather.19.cloned.1.call-update
  27.2 0.5 all-gather.9.cloned.1.call-update
  27.8 0.5 all-gather.17.cloned.1.call-update
  28.4 0.2 convert_reduce_fusion
  28.5 76.5 %all-gather.15.cloned.1.call-done = bf16[256,4096]{1,0:T(8,128)(2,1)} async-done(((bf16[32,4096]{1,0:T(8,128)(2,1)}), bf16[256,4096]{1,0:T(8,128)(2,1)}) %all-gather.15.cloned.1.call-update) | async-done | bytes 2097168 | tf_op jit(solution)/shard_map/all_gather | solution.py:106
  105.0 2.5 convolution_convert_fusion.10
  107.5 3.2 convolution_convert_fusion
  110.9 0.2 convert_reduce_fusion.1
  111.0 68.4 %all-gather.13.cloned.1.call-done = bf16[256,4096]{1,0:T(8,128)(2,1)} async-done(((bf16[32,4096]{1,0:T(8,128)(2,1)}), bf16[256,4096]{1,0:T(8,128)(2,1)}) %all-gather.13.cloned.1.call-update) | async-done | bytes 2097168 | tf_op jit(solution)/shard_map/all_gather | solution.py:105
  179.4 2.5 convolution_convert_fusion.11
  182.0 3.2 convolution_convert_fusion.1
  185.2 0.0 reduce-scatter.7.cloned.1.call-start
  185.3 0.2 convert_reduce_fusion.2
  185.5 69.0 %all-gather.11.cloned.1.call-done = bf16[256,4096]{1,0:T(8,128)(2,1)} async-done(((bf16[32,4096]{1,0:T(8,128)(2,1)}), bf16[256,4096]{1,0:T(8,128)(2,1)}) %all-gather.11.cloned.1.call-update) | async-done | bytes 2097168 | tf_op jit(solution)/shard_map/all_gather | solution.py:102
  254.5 2.2 fusion.2
  256.7 2.4 fusion.20
  259.1 2.3 convolution_convert_fusion.2
  261.4 67.4 %all-gather.19.cloned.1.call-done = bf16[1,256,4096]{2,1,0:T(8,128)(2,1)} async-done(((bf16[1,32,4096]{2,1,0:T(8,128)(2,1)}), bf16[1,256,4096]{2,1,0:T(8,128)(2,1)}) %all-gather.19.cloned.1.call-update) | async-done | bytes 2097168 | tf_op jit(solution)/shard_map/all_gather | solution.py:104
  328.8 2.2 fusion.6
  331.0 0.8 convolution_convert_fusion.9
  331.8 2.3 convolution_convert_fusion.5
  334.1 0.5 stack.9
  334.7 2.6 convolution_convert_fusion.6
  337.3 1.6 pad_maximum_fusion
  338.8 6.4 all-to-all-start
  345.2 0.2 reduce-scatter.5.cloned.1.call-start
  345.4 0.2 convert_reduce_fusion.3
  345.6 72.0 %all-gather.9.cloned.1.call-done = bf16[256,4096]{1,0:T(8,128)(2,1)} async-done(((bf16[32,4096]{1,0:T(8,128)(2,1)}), bf16[256,4096]{1,0:T(8,128)(2,1)}) %all-gather.9.cloned.1.call-update) | async-done | bytes 2097168 | tf_op jit(solution)/shard_map/all_gather | solution.py:101
  417.7 2.2 fusion
  419.9 2.4 fusion.17
  422.3 3.5 convolution_convert_fusion.3
  425.9 0.2 fusion.66
  426.0 0.2 fusion.65
  426.2 65.8 %all-gather.17.cloned.1.call-done = bf16[1,256,4096]{2,1,0:T(8,128)(2,1)} async-done(((bf16[1,32,4096]{2,1,0:T(8,128)(2,1)}), bf16[1,256,4096]{2,1,0:T(8,128)(2,1)}) %all-gather.17.cloned.1.call-update) | async-done | bytes 2097168 | tf_op jit(solution)/shard_map/all_gather | solution.py:103
  492.1 2.2 fusion.4
  494.3 2.5 convolution_convert_fusion.8
  496.8 2.1 convolution_convert_fusion.7
  498.9 2.3 convolution_convert_fusion.4
  501.3 1.5 rev.4
  502.7 6.4 all-to-all-start.1
  509.1 97.1 %reduce-scatter.11.cloned.1.call-done = bf16[32,4096]{1,0:T(8,128)(2,1)} async-done(((bf16[256,4096]{1,0:T(8,128)(2,1)}), bf16[32,4096]{1,0:T(8,128)(2,1)}) %reduce-scatter.11.cloned.1.call-update) | async-done | bytes 262160 | tf_op jit(solution)/shard_map/reduce_scatter | solution.py:42
  606.2 1.2 fusion.61
  607.4 94.4 %reduce-scatter.9.cloned.1.call-done = bf16[32,4096]{1,0:T(8,128)(2,1)} async-done(((bf16[256,4096]{1,0:T(8,128)(2,1)}), bf16[32,4096]{1,0:T(8,128)(2,1)}) %reduce-scatter.9.cloned.1.call-update) | async-done | bytes 262160 | tf_op jit(solution)/shard_map/reduce_scatter | solution.py:42
  701.9 1.3 fusion.57
  703.1 94.3 %reduce-scatter.7.cloned.1.call-done = bf16[32,4096]{1,0:T(8,128)(2,1)} async-done(((bf16[256,4096]{1,0:T(8,128)(2,1)}), bf16[32,4096]{1,0:T(8,128)(2,1)}) %reduce-scatter.7.cloned.1.call-update) | async-done | bytes 262160 | tf_op jit(solution)/shard_map/reduce_scatter | solution.py:42
  797.4 1.8 fusion.68
  799.2 94.2 %reduce-scatter.5.cloned.1.call-done = bf16[32,4096]{1,0:T(8,128)(2,1)} async-done(((bf16[256,4096]{1,0:T(8,128)(2,1)}), bf16[32,4096]{1,0:T(8,128)(2,1)}) %reduce-scatter.5.cloned.1.call-update) | async-done | bytes 262160 | tf_op jit(solution)/shard_map/reduce_scatter | solution.py:42
  893.5 1.8 fusion.67
  895.2 1.9 fusion.69
  897.2 2.0 fusion.70
  899.2 1.9 slice_convert_fusion
  901.1 1.7 reshape.95
  902.9 3.1 fusion.12
  906.0 1.5 add_bitcast_fusion
  (45 shorter events, 0.5 us)
Async XLA Ops:
  7.2 97.8 %all-gather.15.cloned.1.call-start = ((), (), s32[]{:S(2)}) async-start(), calls=%async_computation.12 | async-start | bytes 2359296 | tf_op jit(solution)/shard_map/all_gather | solution.py:106
  7.2 12.1 %collective-permute-start = (bf16[32,4096]{1,0:T(8,128)(2,1)}, bf16[32,4096]{1,0:T(8,128)(2,1)S(1)}, u32[]{:S(2)}, u32[]{:S(2)}) collective-permute-start(bf16[32,4096]{1,0:T(8,128)(2,1)} %bitcast.111), channel_id=1, source_target_pairs={{0,8},{8,16},{16,24},{24,32},{32,40},{40,48},{48,56},{56,64},{64,7... | collective-permute-start | bytes 786440 | tf_op jit(solution)/shard_map/ppermute | solution.py:12
  11.7 7.9 collective-permute-start.1
  13.7 8.8 collective-permute-start.2
  15.6 7.3 collective-permute-start.3
  19.3 9.1 copy-start.9
  19.3 85.7 %copy-start.2 = (bf16[1,2,128,4096]{3,2,1,0:T(8,128)(2,1)S(1)}, bf16[1,2,128,4096]{3,2,1,0:T(8,128)(2,1)}, u32[]{:S(2)}) copy-start(bf16[1,2,128,4096]{3,2,1,0:T(8,128)(2,1)} %param.19) | copy-start | bytes 6291460
  25.1 154.4 %all-gather.13.cloned.1.call-start = ((), (), s32[]{:S(2)}) async-start(), calls=%async_computation.10 | async-start | bytes 2359296 | tf_op jit(solution)/shard_map/all_gather | solution.py:105
  25.8 228.6 %all-gather.11.cloned.1.call-start = ((), (), s32[]{:S(2)}) async-start(), calls=%async_computation.8 | async-start | bytes 2359296 | tf_op jit(solution)/shard_map/all_gather | solution.py:102
  26.6 302.2 %all-gather.19.cloned.1.call-start = ((), (), s32[]{:S(2)}) async-start(), calls=%async_computation.15 | async-start | bytes 2359296 | tf_op jit(solution)/shard_map/all_gather | solution.py:104
  27.1 390.5 %all-gather.9.cloned.1.call-start = ((), (), s32[]{:S(2)}) async-start(), calls=%async_computation.6 | async-start | bytes 2359296 | tf_op jit(solution)/shard_map/all_gather | solution.py:101
  27.7 464.3 %all-gather.17.cloned.1.call-start = ((), (), s32[]{:S(2)}) async-start(), calls=%async_computation.14 | async-start | bytes 2359296 | tf_op jit(solution)/shard_map/all_gather | solution.py:103
  28.3 577.9 %reduce-scatter.11.cloned.1.call-start = ((), (), s32[]{:S(2)}) async-start(), calls=%async_computation.13 | async-start | bytes 2359296 | tf_op jit(solution)/shard_map/reduce_scatter | solution.py:42
  110.8 591.0 %reduce-scatter.9.cloned.1.call-start = ((), (), s32[]{:S(2)}) async-start(), calls=%async_computation.11 | async-start | bytes 2359296 | tf_op jit(solution)/shard_map/reduce_scatter | solution.py:42
  185.2 612.2 %reduce-scatter.7.cloned.1.call-start = ((), (), s32[]{:S(2)}) async-start(), calls=%async_computation.9 | async-start | bytes 2359296 | tf_op jit(solution)/shard_map/reduce_scatter | solution.py:42
  254.5 2.2 copy-start.3
  261.3 69.7 %copy-start.4 = (bf16[1,2,4096,128]{3,2,1,0:T(8,128)(2,1)S(1)}, bf16[1,2,4096,128]{3,2,1,0:T(8,128)(2,1)}, u32[]{:S(2)}) copy-start(bf16[1,2,4096,128]{3,2,1,0:T(8,128)(2,1)} %param.18) | copy-start | bytes 6291460
  328.8 2.3 copy-start.8
  338.8 162.4 %all-to-all-start = ((bf16[2,32,128,128]{3,2,0,1:T(8,128)(2,1)}), bf16[2,32,128,128]{3,2,0,1:T(8,128)(2,1)S(1)}, u32[]{:S(2)}, u32[]{:S(2)}) async-start(bf16[2,32,128,128]{3,2,0,1:T(8,128)(2,1)} %pad_maximum_fusion), calls=%async_computation.4 | async-start | bytes 4194304 | tf_op jit(solution)/shard_map/all_to_all | solution.py:140
  345.2 548.2 %reduce-scatter.5.cloned.1.call-start = ((), (), s32[]{:S(2)}) async-start(), calls=%async_computation.7 | async-start | bytes 2359296 | tf_op jit(solution)/shard_map/reduce_scatter | solution.py:42
  417.7 2.2 copy-start.5
  422.3 3.6 copy-start
  422.3 3.7 copy-start.1
  492.1 2.2 copy-start.6
  494.3 2.5 copy-start.7
  502.7 396.5 %all-to-all-start.1 = ((bf16[2,32,128,128]{3,2,0,1:T(8,128)(2,1)}), bf16[2,32,128,128]{3,2,0,1:T(8,128)(2,1)S(1)}, u32[]{:S(2)}, u32[]{:S(2)}) async-start(bf16[2,32,128,128]{3,2,0,1:T(8,128)(2,1)} %rev.4), calls=%async_computation.5 | async-start | bytes 4194304 | tf_op jit(solution)/shard_map/all_to_all | solution.py:142
Sparse Core Ops, SparseCore 0:
  25.2 79.7 all-gather.14
  107.6 71.7 all-gather.12
  182.6 71.7 all-gather.10
  256.9 71.7 all-gather.18
  331.8 85.8 all-gather.8
  420.1 71.8 all-gather.16
  496.1 110.0 reduce-scatter.10
  610.8 90.9 reduce-scatter.8
  706.5 90.8 reduce-scatter.6
  802.4 90.9 reduce-scatter.4
where the time goes:
time: 916 us; the launch traced here: 914 us
  waiting for transfers between devices  806 us (88%)
  matrix products  34.7 us (4%)
  other arithmetic  30.3 us (3%)
  starting transfers between devices  25.3 us (3%)
  between operations  14.5 us (2%)
    reduce_scatter x4, waiting for transfers between devices, tensor_sum(): lax.psum_scatter(partial_term.astype(jnp.bfloat16), 'tensor', scatter_dim...  380 us
    all_gather x1, waiting for transfers between devices, local(): lax.all_gather(up_upstream, 'tensor', axis=0, tiled=True)  76.5 us
    all_gather x1, waiting for transfers between devices, local(): lax.all_gather(down_input, 'tensor', axis=0, tiled=True)  72 us
    all_gather x1, waiting for transfers between devices, local(): lax.all_gather(up_input, 'tensor', axis=0, tiled=True)  69 us
    all_gather x1, waiting for transfers between devices, local(): lax.all_gather(down_upstream, 'tensor', axis=0, tiled=True)  68.4 us
    all_gather x1, waiting for transfers between devices, local(): lax.all_gather(up_stash[0], 'tensor', axis=0, tiled=True)  67.4 us
    all_gather x1, waiting for transfers between devices, local(): lax.all_gather(down_stash[0], 'tensor', axis=0, tiled=True)  65.8 us
    dot_general x8, matrix products, contract(): lax.dot_general(left_side, right_side, (((left_dim,), (right_dim,)), ((),...  20.9 us
  transfers between devices with their start and end apart: 16, of which 13 were waited for; matrix products, arithmetic and copies ran while one was open for 6% of the time, Pallas kernels for 0%

commit v1 on v0

v1 whole, which is shorter than its diff:
```python
import jax
import jax.numpy as jnp
from jax import lax
from jax.experimental import pallas as pl
from jax.experimental.pallas import tpu as pltpu
from jax.sharding import PartitionSpec as P

eps = 1e-05

RANKS = 32
LANES = 8
RING = 4
ROWS = 32
HALF = RING * ROWS
TOKENS = 2 * HALF
HEAD = 128
WIDTH = 4096
PART = WIDTH // RING
BF16 = jnp.bfloat16
F32 = jnp.float32


def spot(rank, row, half):
    return (rank % RANKS) * LANES + (row % RING) * 2 + half % 2


def moved(shard, rank_to, half_by=0):
    pairs = [
        (spot(r, y, z), spot(rank_to(r), y, z + half_by))
        for r in range(RANKS)
        for y in range(RING)
        for z in range(2)
    ]
    return lax.ppermute(shard, ("pipe", "tensor"), pairs)


def stay(r):
    return r


def up_one(r):
    return r + 1


def down_one(r):
    return r - 1


def mirror(r):
    return RANKS - 1 - r


def mirror_next(r):
    return RANKS - 2 - r


def turned(blocks):
    return lax.all_to_all(
        blocks,
        "tensor",
        split_axis=0,
        concat_axis=0,
        axis_index_groups=[[0, 2, 4, 6], [1, 3, 5, 7]],
        tiled=True,
    )


def after(array, earlier):
    return lax.optimization_barrier((array, earlier))[0]


def block(shape, *index):
    return pl.BlockSpec(shape, lambda i: index)


def whole(array):
    rank = array.ndim
    return pl.BlockSpec(array.shape, lambda i: (0,) * rank)


SCALARS = pl.BlockSpec(memory_space=pltpu.SMEM)


def run(kernel, outs, operands, filled=None, beside=False):
    pairs = [o if isinstance(o, tuple) else (o, whole(o)) for o in operands]
    outs = [o if isinstance(o, tuple) else (o, whole(o)) for o in outs]
    body = kernel
    if filled is not None:
        pairs = [(filled, pl.BlockSpec(memory_space=pl.ANY))] + pairs

        def body(_, *refs):
            kernel(*refs)

    return pl.pallas_call(
        body,
        grid=(1,),
        out_shape=[o for o, _ in outs],
        in_specs=[spec for _, spec in pairs],
        out_specs=[spec for _, spec in outs],
        input_output_aliases={} if filled is None else {0: 0},
        compiler_params=pltpu.CompilerParams(vmem_limit_bytes=63 * 1024 * 1024),
        cost_estimate=pl.CostEstimate(
            flops=10**11 if beside else 1, bytes_accessed=1, transcendentals=0
        ),
    )(*[array for array, _ in pairs])


def out(shape, dtype=BF16):
    return jax.ShapeDtypeStruct(shape, dtype)


def dot(left, right, left_dim=1, right_dim=0):
    return lax.dot_general(
        left, right, (((left_dim,), (right_dim,)), ((), ())), preferred_element_type=F32
    )


def inverse_of(x):
    return lax.rsqrt(jnp.mean(x * x, axis=-1, keepdims=True) + eps)


def columns(ref, row, count, rows):
    for q in range(RING):
        ref[q, row : row + count, :] = rows[:, q * PART : (q + 1) * PART]


def flat(ref):
    return ref[...].reshape(HALF, PART)


def heads(ref):
    return jnp.concatenate([ref[h] for h in range(RING)], axis=1)


def send_kernel(
    place,
    down_prev,
    up_prev,
    down_stash,
    up_stash,
    down_cot,
    up_cot,
    boundary,
    up_ids,
    output_weight,
    below,
    above,
    down_normed,
    up_normed,
    cots,
):
    for stash, normed in ((down_stash, down_normed), (up_stash, up_normed)):
        x = stash[0].astype(F32)
        normed[:, :WIDTH] = (x * inverse_of(x)).astype(BF16)
    up_normed[:, WIDTH:] = up_ids[...]
    columns(cots, 0, HEAD, output_weight[0, 0])
    first = place[0] == 0
    last = place[0] == RANKS - 1

    def choose(edge, index, usual, ref, row, columns_row=None):
        def write(rows):
            ref[row : row + ROWS, :] = rows
            if columns_row is not None:
                columns(cots, columns_row, ROWS, rows)

        @pl.when(edge)
        def _():
            write(boundary[index])

        @pl.when(jnp.logical_not(edge))
        def _():
            write(usual[0])

    choose(last, 0, down_prev, below, 0)
    choose(last, 3, up_cot, below, ROWS, HEAD + ROWS)
    choose(first, 1, up_prev, above, 0)
    choose(first, 2, down_cot, above, ROWS, HEAD)


def inputs_kernel(below, above, n0, n1, n2, n3, sent):
    for i, rows in enumerate((below, above)):
        x = rows[...].astype(F32)
        columns(sent, i * ROWS, ROWS, (x * inverse_of(x)).astype(BF16))
    for i, rows in enumerate((n0, n1, n2, n3)):
        columns(sent, (2 + i) * ROWS, ROWS, rows[:, :WIDTH])


def value_in_kernel(value_weight, sums):
    for q in range(RING):
        sums[q] = value_weight[0, 0, q * PART : (q + 1) * PART, :]


def scaled_kernel(g0, g1, g2, g3, output_cols, sums):
    weights = output_cols[...].reshape(RING * HEAD, PART)
    for i, g in enumerate((g0, g1, g2, g3)):
        parts = dot(flat(g), weights, 1, 1).astype(BF16)
        for h in range(RING):
            sums[h, i * HALF : (i + 1) * HALF, :] = parts[:, h * HEAD : (h + 1) * HEAD]


def token_of(place, dim):
    i = lax.broadcasted_iota(jnp.int32, (TOKENS, TOKENS), dim)
    half = ((i >> 7) + place[1]) & 1
    return (((i >> 5) & 3) * 2 + half) * ROWS + (i & 31)


def mask_kernel(place, ids_row, ids_col, allowed, back):
    rows, cols = token_of(place, 0), token_of(place, 1)
    for job in range(4):
        same = ids_col[:, job : job + 1] == ids_row[job : job + 1, :]
        allowed[job] = jnp.where(jnp.logical_and(rows >= cols, same), 1.0, 0.0).astype(BF16)
        if job >= 2:
            back[job - 2] = jnp.where(jnp.logical_and(cols >= rows, same), 1.0, 0.0).astype(BF16)


def counts_of(allowed):
    return jnp.sum(allowed.astype(F32), axis=1, keepdims=True)


def ring_sum(ref, job):
    rows = slice(job * TOKENS, (job + 1) * TOKENS)
    total = ref[0, rows, :].astype(F32)
    for h in range(1, RING):
        total = total + ref[h, rows, :].astype(F32)
    return total


def act_kernel(allowed, back, sums, acts):
    for job in range(2):
        scaled = (ring_sum(sums, job) / counts_of(allowed[2 + job])).astype(BF16)
        act = dot(back[job], scaled).astype(BF16)
        for h in range(RING):
            acts[h, job * TOKENS : (job + 1) * TOKENS, :] = act


def value_parts(pieces, value_cols, ref, row):
    rows = jnp.concatenate([flat(piece) for piece in pieces], axis=0)
    for h in range(RING):
        ref[h, row : row + 2 * TOKENS, :] = dot(rows, value_cols[h]).astype(BF16)


def values_kernel(x0, x1, x2, x3, value_cols, sums):
    value_parts((x0, x1, x2, x3), value_cols, sums, 0)


def split_home(total, down_own, down_other, up_own, up_other):
    for i, ref in enumerate((down_own, down_other, up_own, up_other)):
        piece = total[i * HALF : (i + 1) * HALF, :].reshape(RING, ROWS, PART)
        ref[...] = piece.astype(ref.dtype)


def normed_grad_kernel(acts, value_cols, *refs):
    split_home(dot(heads(acts), heads(value_cols), 1, 1), *refs)


def added_kernel(mixes, output_cols, *refs):
    weights = output_cols[...].reshape(RING * HEAD, PART)
    split_home(dot(heads(mixes), weights), *refs)


def mixed_kernel(allowed, first, second, mixes):
    for job in range(4):
        values = first if job < 2 else second
        summed = ring_sum(values, job % 2).astype(BF16)
        mix = (dot(allowed[job], summed) / counts_of(allowed[job])).astype(BF16)
        for h in range(RING):
            mixes[h, job * TOKENS : (job + 1) * TOKENS, :] = mix


def grad_kernel(p0, p1, p2, p3, acts, sums):
    rows = jnp.concatenate([flat(piece) for piece in (p0, p1, p2, p3)], axis=0)
    grad = dot(heads(acts), rows, 0, 0).astype(BF16)
    sums[...] = grad.reshape(RING, HEAD, PART)


def sum_kernel(own, other, up_own, up_other, sums):
    sums[:, :ROWS, :] = (own[...] + other[...].astype(F32)).astype(BF16)
    sums[:, ROWS:, :] = (up_own[...].astype(F32) + up_other[...].astype(F32)).astype(BF16)


def value_out_kernel(got, grad):
    for q in range(RING):
        grad[0, q * PART : (q + 1) * PART, :] = got[q].astype(F32).T


def output_out_kernel(got, grad):
    for q in range(RING):
        grad[0, :, q * PART : (q + 1) * PART] = got[q].astype(F32)


def rows_at(got, row):
    return jnp.concatenate([got[q, row : row + ROWS, :] for q in range(RING)], axis=1).astype(F32)


def backward_out_kernel(got, down_grad, up_grad, down_stash, up_stash, down_back, up_back):
    for i, (own_grad, stash, back) in enumerate(
        ((down_grad, down_stash, down_back), (up_grad, up_stash, up_back))
    ):
        normed_grad = rows_at(got, i * ROWS)
        x = stash[0].astype(F32)
        inverse = inverse_of(x)
        normed = x * inverse
        project = jnp.mean(normed_grad * normed, axis=-1, keepdims=True)
        back[0] = (
            own_grad[...].astype(F32) + inverse * (normed_grad - normed * project)
        ).astype(BF16)


def forward_out_kernel(got, down_in, up_in, down_out, up_out):
    down_out[0] = (down_in[...].astype(F32) + rows_at(got, 0)).astype(BF16)
    up_out[0] = (up_in[...].astype(F32) + rows_at(got, ROWS)).astype(BF16)


def home(pieces):
    own, other, up_own, up_other = pieces
    return own, moved(other, stay, 1), moved(up_own, mirror), moved(up_other, mirror, 1)


def local(
    down_prev,
    up_prev,
    down_stash,
    up_stash,
    down_cot,
    up_cot,
    boundary,
    segment_ids,
    value_weight,
    output_weight,
):
    half = lax.axis_index("tensor") % 2
    place = jnp.stack([lax.axis_index("pipe"), half]).astype(jnp.int32)
    placed = (place, SCALARS)
    rows32 = (ROWS, WIDTH)
    cols32 = (RING, ROWS, PART)

    wide = (RING, PART + 2 * TOKENS, HEAD)
    wide_first = block((RING, PART, HEAD), 0, 0, 0)
    wide_last = block((RING, 2 * TOKENS, HEAD), 0, 2, 0)
    lower = block((RING, 2 * TOKENS, HEAD), 0, 0, 0)
    upper = block((RING, 2 * TOKENS, HEAD), 0, 1, 0)

    wide = out((RING, PART + 2 * TOKENS, HEAD))
    narrow, double = out((RING, 2 * TOKENS, HEAD)), out((RING, 4 * TOKENS, HEAD))
    lower, upper, last = (block((RING, 2 * TOKENS, HEAD), 0, i, 0) for i in range(3))
    first = block((RING, PART, HEAD), 0, 0, 0)

    up_ids = jnp.pad(segment_ids[1::2, 0].reshape(4, HEAD), ((0, ROWS - 4), (0, 0))).astype(BF16)

    below_sent, above_sent, down_n, up_n, cots = run(
        send_kernel,
        [
            out((2 * ROWS, WIDTH)),
            out((2 * ROWS, WIDTH)),
            out(rows32),
            out((ROWS, WIDTH + HEAD)),
            out((RING, HEAD + 2 * ROWS, PART)),
        ],
        [
            placed,
            down_prev,
            up_prev,
            down_stash,
            up_stash,
            down_cot,
            up_cot,
            boundary,
            up_ids,
            (output_weight, block((1, 1, HEAD, WIDTH), 0, 0, 0, 0)),
        ],
    )
    kept_rows = (down_n, moved(down_n, stay, 1), moved(up_n, mirror), moved(up_n, mirror, 1))
    below = moved(below_sent, up_one)
    above = moved(above_sent, down_one)

    cots = turned(cots)
    output_cols = (cots, block((RING, HEAD, PART), 0, 0, 0))
    down_g, up_g = cots[:, HEAD : HEAD + ROWS], cots[:, HEAD + ROWS :]
    grads = (
        moved(down_g, down_one),
        moved(down_g, down_one, 1),
        moved(up_g, mirror_next),
        moved(up_g, mirror_next, 1),
    )

    sent = run(
        inputs_kernel,
        [out((RING, 6 * ROWS, PART))],
        [(below, block(rows32, 0, 0)), (above, block(rows32, 0, 0)), *kept_rows],
    )[0]
    sent = turned(after(sent, cots))
    kept = [(sent, block(cols32, 0, 2 + i, 0)) for i in range(4)]
    down_x, up_x = sent[:, :ROWS], sent[:, ROWS : 2 * ROWS]
    inputs = (
        (sent, block(cols32, 0, 0, 0)),
        moved(down_x, stay, 1),
        moved(up_x, mirror),
        moved(up_x, mirror, 1),
    )

    mirrored = kept_rows[2][:4, WIDTH:].astype(jnp.int32).reshape(2, TOKENS)
    ids = jnp.stack([segment_ids[0, 0], mirrored[0], segment_ids[2, 0], mirrored[1]])
    by_half = ids.reshape(4, RING, 2, ROWS).transpose(0, 2, 1, 3)
    ids_row = jnp.where(half == 0, by_half, by_half[:, ::-1]).reshape(4, TOKENS)
    ids_col = ids_row.T
    square = (TOKENS, TOKENS)
    allowed, allowed_back = run(
        mask_kernel, [out((4, *square)), out((2, *square))], [placed, ids_row, ids_col], beside=True
    )

    got3 = run(
        value_in_kernel,
        [(wide, first)],
        [(after(value_weight, cots), block((1, 1, WIDTH, HEAD), 0, 0, 0, 0))],
        beside=True,
    )[0]
    got3 = run(scaled_kernel, [(wide, last)], [*grads, output_cols], filled=got3)[0]
    got3 = turned(after(got3, sent))
    value_cols = (got3, first)

    acts = run(act_kernel, [narrow], [allowed, allowed_back, (got3, last)])[0]
    acts = turned(after(acts, inputs[1:]))
    pieces = [out(cols32, F32), out(cols32), out(cols32), out(cols32)]
    normed_grads = run(normed_grad_kernel, pieces, [acts, value_cols])
    ready = normed_grads[1]
    normed_grads = home(normed_grads)

    values = run(values_kernel, [(double, upper)], [*kept, value_cols])[0]
    values = after(values, ready)
    values = turned(
        run(values_kernel, [(double, lower)], [*inputs, value_cols], filled=values)[0]
    )

    mixes = turned(run(mixed_kernel, [double], [allowed, (values, lower), (values, upper)])[0])
    added = run(added_kernel, pieces, [(mixes, lower), output_cols])
    ready = added[1]
    added = home(added)

    tall = out((RING, 2 * HEAD + 2 * ROWS, PART))
    value_part, output_part = (block((RING, HEAD, PART), 0, i, 0) for i in range(2))
    rows_part = block((RING, 2 * ROWS, PART), 0, 4, 0)
    sums = run(grad_kernel, [(tall, value_part)], [*kept, acts], beside=True)[0]
    sums = run(sum_kernel, [(tall, rows_part)], [*normed_grads], filled=sums, beside=True)[0]
    sums = turned(
        run(
            grad_kernel,
            [(tall, output_part)],
            [*grads, (after(mixes, ready), upper)],
            filled=sums,
        )[0]
    )
    value_grad = run(value_out_kernel, [out((1, WIDTH, HEAD), F32)], [(sums, value_part)])[0]
    output_grad = run(output_out_kernel, [out((1, HEAD, WIDTH), F32)], [(sums, output_part)])[0]
    lower_rows, upper_rows = (block(rows32, i, 0) for i in range(2))
    down_back, up_back = run(
        backward_out_kernel,
        [out((1, ROWS, WIDTH))] * 2,
        [(sums, rows_part), (above, upper_rows), (below, upper_rows), down_stash, up_stash],
    )

    rows = turned(after(run(sum_kernel, [out((RING, 2 * ROWS, PART))], [*added])[0], sums))
    down_out, up_out = run(
        forward_out_kernel,
        [out((1, ROWS, WIDTH))] * 2,
        [rows, (below, lower_rows), (above, lower_rows)],
    )
    return down_out, up_out, down_back, up_back, value_grad, output_grad


def solution(mesh):
    placed = (
        P("pipe", "tensor", None),
        P("pipe", "tensor", None),
        P("pipe", "tensor", None),
        P("pipe", "tensor", None),
        P("pipe", "tensor", None),
        P("pipe", "tensor", None),
        P(None, "tensor", None),
        P(None, "pipe", None),
        P("pipe", None, None, "tensor"),
        P("pipe", None, "tensor", None),
    )
    return jax.shard_map(
        local,
        mesh=mesh,
        in_specs=placed,
        out_specs=(
            P("pipe", "tensor", None),
            P("pipe", "tensor", None),
            P("pipe", "tensor", None),
            P("pipe", "tensor", None),
            P("pipe", None, "tensor"),
            P("pipe", "tensor", None),
        ),
        check_vma=False,
    )
```

time: 916 us -> 254 us (0.28)
  waiting for transfers between devices: 806 us -> 88.3 us
  starting transfers between devices: 25.3 us -> 95.8 us
  Pallas kernels: 0 us -> 54.4 us
  matrix products: 34.7 us -> 0 us
  other arithmetic: 30.3 us -> 1.31 us
  between operations: 14.5 us -> 0.86 us
    all_gather x6 -> x0, waiting for transfers between devices: 419 us -> none  [the longest x1 76.5 us: local(): lax.all_gather(up_upstream, 'tensor', axis=0, tiled=True)]
    reduce_scatter x4 -> x0, waiting for transfers between devices: 380 us -> none  [tensor_sum(): lax.psum_scatter(partial_term.astype(jnp.bfloat16), 'tensor', scatter_dim...]
    ppermute x4 -> x18, waiting for transfers between devices: 3.57 us -> 66.7 us  [moved(): return lax.ppermute(shard, ('pipe', 'tensor'), pairs)]
    pallas_call x0 -> x19, Pallas kernels: none -> 54.4 us  [run(): pl.pallas_call(body, grid=(1,), out_shape=[o for o, _ in outs], in_specs=...]
    ppermute x4 -> x18, starting transfers between devices: 12 us -> 60.9 us  [moved(): return lax.ppermute(shard, ('pipe', 'tensor'), pairs)]
    dot_general x14 -> x0, matrix products: 34.7 us -> none  [the longest x8 20.9 us: contract(): lax.dot_general(left_side, right_side, (((left_dim,), (right_dim,)), ((),...]
    all_to_all x2 -> x8, starting transfers between devices: 12.7 us -> 34.9 us  [turned(): lax.all_to_all(blocks, 'tensor', split_axis=0, concat_axis=0, axis_index_...]
    all_to_all x2 -> x8, waiting for transfers between devices: 0.01 us -> 21.6 us  [turned(): lax.all_to_all(blocks, 'tensor', split_axis=0, concat_axis=0, axis_index_...]
  transfers between devices with their start and end apart: 16 -> 26, of which waited for: 13 -> 15; matrix products, arithmetic and copies ran while one was open for 6% -> 0% of each run, Pallas kernels for 0% -> 15%
where the time goes in v1:
time: 254 us; the launch traced here: 252 us
  starting transfers between devices  95.8 us (38%)
  waiting for transfers between devices  88.3 us (35%)
  Pallas kernels  54.4 us (21%)
  local copies, waits for them, and re-layouts  11.7 us (5%)
    ppermute x18, waiting for transfers between devices, moved(): return lax.ppermute(shard, ('pipe', 'tensor'), pairs)  66.7 us
    ppermute x18, starting transfers between devices, moved(): return lax.ppermute(shard, ('pipe', 'tensor'), pairs)  60.9 us
    pallas_call x19, Pallas kernels, run(): pl.pallas_call(body, grid=(1,), out_shape=[o for o, _ in outs], in_specs=...  54.4 us
    all_to_all x8, starting transfers between devices, turned(): lax.all_to_all(blocks, 'tensor', split_axis=0, concat_axis=0, axis_index_...  34.9 us
    all_to_all x8, waiting for transfers between devices, turned(): lax.all_to_all(blocks, 'tensor', split_axis=0, concat_axis=0, axis_index_...  21.6 us
    unnamed x54, local copies, waits for them, and re-layouts  6.15 us
  transfers between devices with their start and end apart: 26, of which 15 were waited for; matrix products, arithmetic and copies ran while one was open for 0% of the time, Pallas kernels for 15%

profile of v1, /device:TPU:1, one launch (start us, length us, event | category | flops | bytes accessed | tf_op | source)
XLA Modules:
  0.0 252.3 jit_solution(6462588689826292981)
XLA Ops:
  0.6 0.7 convert.6
  2.6 4.1 %shard_map.145 = (bf16[64,4096]{1,0:T(8,128)(2,1)}, bf16[64,4096]{1,0:T(8,128)(2,1)}, bf16[32,4096]{1,0:T(8,128)(2,1)}, bf16[32,4224]{1,0:T(8,128)(2,1)}, bf16[4,192,1024]{2,1,0:T(8,128)(2,1)}) custom-call(s32[2]{0:T(128)} %pad_add_fusion.place, bf16[1,32,4096]{2,1,0:T(8,128)(2,1)} %down_prev.1, bf16[1,32,4096]{2,1,0:T(8,128)(2,1)} %up_prev.1, ...), custom_call_target="tpu_custom_call" | custom-call | flops 1 | bytes 1 | tf_op jit(solution)/shard_map/pallas_call | solution.py:94
  6.7 5.2 %all-to-all-start = ((bf16[4,192,1024]{2,1,0:T(8,128)(2,1)}), bf16[4,192,1024]{2,1,0:T(8,128)(2,1)}, u32[]{:S(2)}, u32[]{:S(2)}) async-start(bf16[4,192,1024]{2,1,0:T(8,128)(2,1)} %get-tuple-element.37), calls=%async_computation | async-start | bytes 3145728 | tf_op jit(solution)/shard_map/all_to_all | solution.py:58
  11.8 7.4 %collective-permute-start = (bf16[32,4224]{1,0:T(8,128)(2,1)S(1)}, bf16[32,4224]{1,0:T(8,128)(2,1)S(1)}, u32[]{:S(2)}, u32[]{:S(2)}) collective-permute-start(bf16[32,4224]{1,0:T(8,128)(2,1)S(1)} %copy-done.20), channel_id=1, source_target_pairs={{0,248},{1,249},{2,250},{3,251},{4,252},{5,253},{6,254},{7,255},{8... | collective-permute-start | bytes 811016 | tf_op jit(solution)/shard_map/ppermute | solution.py:34
  19.2 2.5 collective-permute-start.4
  21.7 1.7 collective-permute-start.3
  24.1 4.7 %collective-permute-done.n2 = bf16[32,4224]{1,0:T(8,128)(2,1)S(1)} collective-permute-done((bf16[32,4224]{1,0:T(8,128)(2,1)S(1)}, bf16[32,4224]{1,0:T(8,128)(2,1)S(1)}, u32[]{:S(2)}, u32[]{:S(2)}) %collective-permute-start) | collective-permute-done | bytes 270368 | tf_op jit(solution)/shard_map/ppermute | solution.py:34
  29.9 12.4 %collective-permute-done.3.n1 = bf16[32,4096]{1,0:T(8,128)(2,1)S(1)} collective-permute-done((bf16[32,4096]{1,0:T(8,128)(2,1)S(1)}, bf16[32,4096]{1,0:T(8,128)(2,1)S(1)}, u32[]{:S(2)}, u32[]{:S(2)}) %collective-permute-start.3) | collective-permute-done | bytes 262176 | tf_op jit(solution)/shard_map/ppermute | solution.py:34
  42.3 5.3 %collective-permute-done.4.n3 = bf16[32,4224]{1,0:T(8,128)(2,1)S(1)} collective-permute-done((bf16[32,4224]{1,0:T(8,128)(2,1)S(1)}, bf16[32,4224]{1,0:T(8,128)(2,1)S(1)}, u32[]{:S(2)}, u32[]{:S(2)}) %collective-permute-start.4) | collective-permute-done | bytes 270368 | tf_op jit(solution)/shard_map/ppermute | solution.py:34
  47.7 0.7 copy-done.8
  48.4 0.8 copy-done
  49.2 2.7 %shard_map.147 = bf16[4,192,1024]{2,1,0:T(8,128)(2,1)} custom-call(bf16[64,4096]{1,0:T(8,128)(2,1)} %copy-done, bf16[64,4096]{1,0:T(8,128)(2,1)} %collective-permute-done.2.above.up_in.down_grad, bf16[32,4096]{1,0:T(8,128)(2,1)} %get-tuple-element.36.n0, bf16[32,4096]{1,0:T(8,128)(2,1)} %copy-done.10, bf16[32,4224]{1,0:T(8,128)(2,1)} %copy-done.7, ...), custom_call_target="tpu_custom_call" | custom-call | flops 1 | bytes 1 | tf_op jit(solution)/shard_map/pallas_call | solution.py:94
  52.0 1.9 fusion.1
  53.8 1.7 collective-permute-start.8
  55.5 6.9 %collective-permute-start.7 = (bf16[4,32,1024]{2,1,0:T(8,128)(2,1)}, bf16[4,32,1024]{2,1,0:T(8,128)(2,1)S(1)}, u32[]{:S(2)}, u32[]{:S(2)}) collective-permute-start(bf16[4,32,1024]{2,1,0:T(8,128)(2,1)} %get-tuple-element.62), channel_id=1, source_target_pairs={{0,240},{1,241},{2,242},{3,243},{4,244},{5,245},{6,246},{7,247},{8... | collective-permute-start | bytes 786440 | tf_op jit(solution)/shard_map/ppermute | solution.py:34
  62.5 1.1 collective-permute-start.6
  63.6 4.3 %all-to-all-start.1 = ((bf16[4,192,1024]{2,1,0:T(8,128)(2,1)}), bf16[4,192,1024]{2,1,0:T(8,128)(2,1)}, u32[]{:S(2)}, u32[]{:S(2)}) async-start(bf16[4,192,1024]{2,1,0:T(8,128)(2,1)} %shard_map.147), calls=%async_computation.1 | async-start | bytes 3145728 | tf_op jit(solution)/shard_map/all_to_all | solution.py:58
  67.9 2.3 shard_map.148._
  70.2 2.6 %collective-permute-done.8.refs_3_ = bf16[4,32,1024]{2,1,0:T(8,128)(2,1)S(1)} collective-permute-done((bf16[4,32,1024]{2,1,0:T(8,128)(2,1)}, bf16[4,32,1024]{2,1,0:T(8,128)(2,1)S(1)}, u32[]{:S(2)}, u32[]{:S(2)}) %collective-permute-start.8) | collective-permute-done | bytes 262176 | tf_op jit(solution)/shard_map/ppermute | solution.py:34
  72.8 8.0 %collective-permute-done.7.refs_2_ = bf16[4,32,1024]{2,1,0:T(8,128)(2,1)S(1)} collective-permute-done((bf16[4,32,1024]{2,1,0:T(8,128)(2,1)}, bf16[4,32,1024]{2,1,0:T(8,128)(2,1)S(1)}, u32[]{:S(2)}, u32[]{:S(2)}) %collective-permute-start.7) | collective-permute-done | bytes 262176 | tf_op jit(solution)/shard_map/ppermute | solution.py:34
  80.8 5.6 %collective-permute-done.6.refs_1_ = bf16[4,32,1024]{2,1,0:T(8,128)(2,1)S(1)} collective-permute-done((bf16[4,32,1024]{2,1,0:T(8,128)(2,1)}, bf16[4,32,1024]{2,1,0:T(8,128)(2,1)S(1)}, u32[]{:S(2)}, u32[]{:S(2)}) %collective-permute-start.6) | collective-permute-done | bytes 262176 | tf_op jit(solution)/shard_map/ppermute | solution.py:34
  87.1 3.8 %shard_map.149 = bf16[4,1536,128]{2,1,0:T(8,128)(2,1)} custom-call(bf16[4,1536,128]{2,1,0:T(8,128)(2,1)} %shard_map.148._, bf16[4,32,1024]{2,1,0:T(8,128)(2,1)} %collective-permute-done.5.refs_0_, bf16[4,32,1024]{2,1,0:T(8,128)(2,1)} %copy-done.5, bf16[4,32,1024]{2,1,0:T(8,128)(2,1)} %copy-done.4, ...), custom_call_target="tpu_custom_call", output_to_operand_aliasing={{}: (0, {})} | custom-call | flops 1 | bytes 1 | tf_op jit(solution)/shard_map/pallas_call | solution.py:94
  91.0 1.9 fusion
  92.9 3.4 %collective-permute-start.10 = (bf16[4,32,1024]{2,1,0:T(8,128)(2,1)}, bf16[4,32,1024]{2,1,0:T(8,128)(2,1)S(1)}, u32[]{:S(2)}, u32[]{:S(2)}) collective-permute-start(bf16[4,32,1024]{2,1,0:T(8,128)(2,1)} %get-tuple-element.60), channel_id=1, source_target_pairs={{0,248},{1,249},{2,250},{3,251},{4,252},{5,253},{6,254},{7,255},{8... | collective-permute-start | bytes 786440 | tf_op jit(solution)/shard_map/ppermute | solution.py:34
  96.3 4.6 %collective-permute-start.9 = (bf16[4,32,1024]{2,1,0:T(8,128)(2,1)}, bf16[4,32,1024]{2,1,0:T(8,128)(2,1)S(1)}, u32[]{:S(2)}, u32[]{:S(2)}) collective-permute-start(bf16[4,32,1024]{2,1,0:T(8,128)(2,1)} %get-tuple-element.61), channel_id=1, source_target_pairs={{0,1},{1,0},{2,3},{3,2},{4,5},{5,4},{6,7},{7,6},{8,9},{9,8},{10,11... | collective-permute-start | bytes 786440 | tf_op jit(solution)/shard_map/ppermute | solution.py:34
  100.9 4.3 %all-to-all-start.2 = ((bf16[4,1536,128]{2,1,0:T(8,128)(2,1)}), bf16[4,1536,128]{2,1,0:T(8,128)(2,1)}, u32[]{:S(2)}, u32[]{:S(2)}) async-start(bf16[4,1536,128]{2,1,0:T(8,128)(2,1)} %shard_map.149), calls=%async_computation.2 | async-start | bytes 3145728 | tf_op jit(solution)/shard_map/all_to_all | solution.py:58
  105.3 2.1 shard_map.146
  107.3 14.5 %all-to-all-done.2.value_cols.sums.refs_4_ = bf16[4,1536,128]{2,1,0:T(8,128)(2,1)} async-done(((bf16[4,1536,128]{2,1,0:T(8,128)(2,1)}), bf16[4,1536,128]{2,1,0:T(8,128)(2,1)}, u32[]{:S(2)}, u32[]{:S(2)}) %all-to-all-start.2) | async-done | bytes 1572896 | tf_op jit(solution)/shard_map/all_to_all | solution.py:58
  121.8 2.4 shard_map.151
  124.3 0.7 copy-done.13
  125.1 3.6 %all-to-all-start.3 = ((bf16[4,512,128]{2,1,0:T(8,128)(2,1)}), bf16[4,512,128]{2,1,0:T(8,128)(2,1)S(1)}, u32[]{:S(2)}, u32[]{:S(2)}) async-start(bf16[4,512,128]{2,1,0:T(8,128)(2,1)} %shard_map.151), calls=%async_computation.3 | async-start | bytes 1048576 | tf_op jit(solution)/shard_map/all_to_all | solution.py:58
  128.7 3.6 %shard_map.150._ = bf16[4,1024,128]{2,1,0:T(8,128)(2,1)} custom-call(bf16[4,192,1024]{2,1,0:T(8,128)(2,1)} %all-to-all-done.1.x0.x1.x2.x3.refs_0_.p0.p1.p2.p3, bf16[4,192,1024]{2,1,0:T(8,128)(2,1)} %all-to-all-done.1.x0.x1.x2.x3.refs_0_.p0.p1.p2.p3, bf16[4,192,1024]{2,1,0:T(8,128)(2,1)} %all-to-all-done.1.x0.x1.x2.x3.refs_0_.p0.p1.p2.p3, ...), custom_call_target="tpu_custom_call" | custom-call | flops 1 | bytes 1 | tf_op jit(solution)/shard_map/pallas_call | solution.py:94
  132.3 3.3 %all-to-all-done.3.acts = bf16[4,512,128]{2,1,0:T(8,128)(2,1)S(1)} async-done(((bf16[4,512,128]{2,1,0:T(8,128)(2,1)}), bf16[4,512,128]{2,1,0:T(8,128)(2,1)S(1)}, u32[]{:S(2)}, u32[]{:S(2)}) %all-to-all-start.3) | async-done | bytes 524320 | tf_op jit(solution)/shard_map/all_to_all | solution.py:58
  135.7 0.8 copy-done.2
  136.4 3.1 %shard_map.152 = (f32[4,32,1024]{2,1,0:T(8,128)}, bf16[4,32,1024]{2,1,0:T(8,128)(2,1)}, bf16[4,32,1024]{2,1,0:T(8,128)(2,1)}, bf16[4,32,1024]{2,1,0:T(8,128)(2,1)}) custom-call(bf16[4,512,128]{2,1,0:T(8,128)(2,1)} %copy-done.2, bf16[4,1536,128]{2,1,0:T(8,128)(2,1)} %all-to-all-done.2.value_cols.sums.refs_4_), custom_call_target="tpu_custom_call" | custom-call | flops 1 | bytes 1 | tf_op jit(solution)/shard_map/pallas_call | solution.py:94
  139.6 2.6 %collective-permute-start.15 = (bf16[4,32,1024]{2,1,0:T(8,128)(2,1)}, bf16[4,32,1024]{2,1,0:T(8,128)(2,1)S(1)}, u32[]{:S(2)}, u32[]{:S(2)}) collective-permute-start(bf16[4,32,1024]{2,1,0:T(8,128)(2,1)} %get-tuple-element.43), channel_id=1, source_target_pairs={{0,1},{1,0},{2,3},{3,2},{4,5},{5,4},{6,7},{7,6},{8,9},{9,8},{10,11... | collective-permute-start | bytes 786440 | tf_op jit(solution)/shard_map/ppermute | solution.py:34
  142.1 3.6 %shard_map.153 = bf16[4,1024,128]{2,1,0:T(8,128)(2,1)} custom-call(bf16[4,1024,128]{2,1,0:T(8,128)(2,1)} %shard_map.150._, bf16[4,192,1024]{2,1,0:T(8,128)(2,1)} %all-to-all-done.1.x0.x1.x2.x3.refs_0_.p0.p1.p2.p3, bf16[4,32,1024]{2,1,0:T(8,128)(2,1)} %copy-done.13, bf16[4,32,1024]{2,1,0:T(8,128)(2,1)} %copy-done.12, ...), custom_call_target="tpu_custom_call", output_to_operand_aliasing={{}: (0, {})} | custom-call | flops 1 | bytes 1 | tf_op jit(solution)/shard_map/pallas_call | solution.py:94
  145.7 4.4 %all-to-all-start.4 = ((bf16[4,1024,128]{2,1,0:T(8,128)(2,1)}), bf16[4,1024,128]{2,1,0:T(8,128)(2,1)}, u32[]{:S(2)}, u32[]{:S(2)}) async-start(bf16[4,1024,128]{2,1,0:T(8,128)(2,1)} %shard_map.153), calls=%async_computation.4 | async-start | bytes 2097152 | tf_op jit(solution)/shard_map/all_to_all | solution.py:58
  150.1 5.1 %collective-permute-start.16 = (bf16[4,32,1024]{2,1,0:T(8,128)(2,1)S(1)}, bf16[4,32,1024]{2,1,0:T(8,128)(2,1)}, u32[]{:S(2)}, u32[]{:S(2)}) collective-permute-start(bf16[4,32,1024]{2,1,0:T(8,128)(2,1)S(1)} %copy-done.23), channel_id=1, source_target_pairs={{0,248},{1,249},{2,250},{3,251},{4,252},{5,253},{6,254},{7,255},{8... | collective-permute-start | bytes 786440 | tf_op jit(solution)/shard_map/ppermute | solution.py:34
  155.2 1.5 collective-permute-start.17
  156.7 3.1 %shard_map.157._ = bf16[4,320,1024]{2,1,0:T(8,128)(2,1)} custom-call(bf16[4,192,1024]{2,1,0:T(8,128)(2,1)} %all-to-all-done.1.x0.x1.x2.x3.refs_0_.p0.p1.p2.p3, bf16[4,192,1024]{2,1,0:T(8,128)(2,1)} %all-to-all-done.1.x0.x1.x2.x3.refs_0_.p0.p1.p2.p3, bf16[4,192,1024]{2,1,0:T(8,128)(2,1)} %all-to-all-done.1.x0.x1.x2.x3.refs_0_.p0.p1.p2.p3, ...), custom_call_target="tpu_custom_call" | custom-call | flops 99999997952 | bytes 1 | tf_op jit(solution)/shard_map/pallas_call | solution.py:94
  159.9 2.7 %shard_map.154 = bf16[4,1024,128]{2,1,0:T(8,128)(2,1)} custom-call(bf16[4,256,256]{2,1,0:T(8,128)(2,1)} %get-tuple-element.33.allowed, bf16[4,1024,128]{2,1,0:T(8,128)(2,1)} %all-to-all-done.4.first.second, bf16[4,1024,128]{2,1,0:T(8,128)(2,1)} %all-to-all-done.4.first.second), custom_call_target="tpu_custom_call" | custom-call | flops 1 | bytes 1 | tf_op jit(solution)/shard_map/pallas_call | solution.py:94
  162.6 4.3 %all-to-all-start.5 = ((bf16[4,1024,128]{2,1,0:T(8,128)(2,1)}), bf16[4,1024,128]{2,1,0:T(8,128)(2,1)}, u32[]{:S(2)}, u32[]{:S(2)}) async-start(bf16[4,1024,128]{2,1,0:T(8,128)(2,1)} %shard_map.154), calls=%async_computation.5 | async-start | bytes 2097152 | tf_op jit(solution)/shard_map/all_to_all | solution.py:58
  166.9 1.3 collective-permute-done.16.refs_2_
  168.2 3.3 %collective-permute-done.17.refs_3_ = bf16[4,32,1024]{2,1,0:T(8,128)(2,1)} collective-permute-done((bf16[4,32,1024]{2,1,0:T(8,128)(2,1)S(1)}, bf16[4,32,1024]{2,1,0:T(8,128)(2,1)}, u32[]{:S(2)}, u32[]{:S(2)}) %collective-permute-start.17) | collective-permute-done | bytes 262176 | tf_op jit(solution)/shard_map/ppermute | solution.py:34
  171.6 0.7 copy-done.21
  172.3 2.2 shard_map.158._
  174.4 2.3 all-to-all-done.5.mixes.refs_4_
  176.7 3.0 %shard_map.155 = (f32[4,32,1024]{2,1,0:T(8,128)}, bf16[4,32,1024]{2,1,0:T(8,128)(2,1)}, bf16[4,32,1024]{2,1,0:T(8,128)(2,1)}, bf16[4,32,1024]{2,1,0:T(8,128)(2,1)}) custom-call(bf16[4,1024,128]{2,1,0:T(8,128)(2,1)} %all-to-all-done.5.mixes.refs_4_, bf16[4,192,1024]{2,1,0:T(8,128)(2,1)} %all-to-all-done.refs_4_.output_cols), custom_call_target="tpu_custom_call" | custom-call | flops 1 | bytes 1 | tf_op jit(solution)/shard_map/pallas_call | solution.py:94
  179.7 3.1 %shard_map.159 = bf16[4,320,1024]{2,1,0:T(8,128)(2,1)} custom-call(bf16[4,320,1024]{2,1,0:T(8,128)(2,1)} %shard_map.158._, bf16[4,32,1024]{2,1,0:T(8,128)(2,1)} %collective-permute-done.5.refs_0_, bf16[4,32,1024]{2,1,0:T(8,128)(2,1)} %copy-done.5, bf16[4,32,1024]{2,1,0:T(8,128)(2,1)} %copy-done.4, ...), custom_call_target="tpu_custom_call", output_to_operand_aliasing={{}: (0, {})} | custom-call | flops 1 | bytes 1 | tf_op jit(solution)/shard_map/pallas_call | solution.py:94
  182.8 4.7 %all-to-all-start.6 = ((bf16[4,320,1024]{2,1,0:T(8,128)(2,1)}), bf16[4,320,1024]{2,1,0:T(8,128)(2,1)}, u32[]{:S(2)}, u32[]{:S(2)}) async-start(bf16[4,320,1024]{2,1,0:T(8,128)(2,1)} %shard_map.159), calls=%async_computation.6 | async-start | bytes 5242880 | tf_op jit(solution)/shard_map/all_to_all | solution.py:58
  187.5 17.4 %collective-permute-start.13 = (bf16[4,32,1024]{2,1,0:T(8,128)(2,1)S(1)}, bf16[4,32,1024]{2,1,0:T(8,128)(2,1)S(1)}, u32[]{:S(2)}, u32[]{:S(2)}) collective-permute-start(bf16[4,32,1024]{2,1,0:T(8,128)(2,1)S(1)} %copy-done.26), channel_id=1, source_target_pairs={{0,248},{1,249},{2,250},{3,251},{4,252},{5,253},{6,254},{7,255},{8... | collective-permute-start | bytes 786440 | tf_op jit(solution)/shard_map/ppermute | solution.py:34
  205.0 1.5 collective-permute-start.14
  206.5 3.0 %collective-permute-start.12 = (bf16[4,32,1024]{2,1,0:T(8,128)(2,1)S(1)}, bf16[4,32,1024]{2,1,0:T(8,128)(2,1)S(1)}, u32[]{:S(2)}, u32[]{:S(2)}) collective-permute-start(bf16[4,32,1024]{2,1,0:T(8,128)(2,1)S(1)} %copy-done.24), channel_id=1, source_target_pairs={{0,1},{1,0},{2,3},{3,2},{4,5},{5,4},{6,7},{7,6},{8,9},{9,8},{10,11... | collective-permute-start | bytes 786440 | tf_op jit(solution)/shard_map/ppermute | solution.py:34
  209.4 4.8 %collective-permute-done.13.up_own = bf16[4,32,1024]{2,1,0:T(8,128)(2,1)S(1)} collective-permute-done((bf16[4,32,1024]{2,1,0:T(8,128)(2,1)S(1)}, bf16[4,32,1024]{2,1,0:T(8,128)(2,1)S(1)}, u32[]{:S(2)}, u32[]{:S(2)}) %collective-permute-start.13) | collective-permute-done | bytes 262176 | tf_op jit(solution)/shard_map/ppermute | solution.py:34
  214.2 18.6 %collective-permute-done.14.up_other = bf16[4,32,1024]{2,1,0:T(8,128)(2,1)S(1)} collective-permute-done((bf16[4,32,1024]{2,1,0:T(8,128)(2,1)S(1)}, bf16[4,32,1024]{2,1,0:T(8,128)(2,1)S(1)}, u32[]{:S(2)}, u32[]{:S(2)}) %collective-permute-start.14) | collective-permute-done | bytes 262176 | tf_op jit(solution)/shard_map/ppermute | solution.py:34
  233.6 2.2 shard_map.156
  235.8 4.1 %all-to-all-start.7 = ((bf16[4,64,1024]{2,1,0:T(8,128)(2,1)}), bf16[4,64,1024]{2,1,0:T(8,128)(2,1)S(1)}, u32[]{:S(2)}, u32[]{:S(2)}) async-start(bf16[4,64,1024]{2,1,0:T(8,128)(2,1)} %shard_map.156), calls=%async_computation.7 | async-start | bytes 1048576 | tf_op jit(solution)/shard_map/all_to_all | solution.py:58
  239.9 2.7 %shard_map.161 = (bf16[1,32,4096]{2,1,0:T(8,128)(2,1)}, bf16[1,32,4096]{2,1,0:T(8,128)(2,1)}) custom-call(bf16[4,320,1024]{2,1,0:T(8,128)(2,1)} %all-to-all-done.6.got, bf16[64,4096]{1,0:T(8,128)(2,1)} %collective-permute-done.2.above.up_in.down_grad, bf16[64,4096]{1,0:T(8,128)(2,1)} %copy-done, bf16[1,32,4096]{2,1,0:T(8,128)(2,1)} %down_stash.3, ...), custom_call_target="tpu_custom_call" | custom-call | flops 1 | bytes 1 | tf_op jit(solution)/shard_map/pallas_call | solution.py:94
  242.6 2.7 %shard_map.163 = f32[1,128,4096]{2,1,0:T(8,128)} custom-call(bf16[4,320,1024]{2,1,0:T(8,128)(2,1)} %all-to-all-done.6.got), custom_call_target="tpu_custom_call" | custom-call | flops 1 | bytes 1 | tf_op jit(solution)/shard_map/pallas_call | solution.py:94
  245.3 2.9 %shard_map.162 = f32[1,4096,128]{2,1,0:T(8,128)} custom-call(bf16[4,320,1024]{2,1,0:T(8,128)(2,1)} %all-to-all-done.6.got), custom_call_target="tpu_custom_call" | custom-call | flops 1 | bytes 1 | tf_op jit(solution)/shard_map/pallas_call | solution.py:94
  248.2 1.3 all-to-all-done.7.got
  249.5 0.8 copy-done.1
  250.3 2.0 shard_map.160
  (80 shorter events, 4.7 us)
Async XLA Ops:
  6.6 5.2 %copy-start.20 = (bf16[32,4224]{1,0:T(8,128)(2,1)S(1)}, bf16[32,4224]{1,0:T(8,128)(2,1)}, u32[]{:S(2)}) copy-start(bf16[32,4224]{1,0:T(8,128)(2,1)} %get-tuple-element.32) | copy-start | bytes 811012
  6.6 15.1 %copy-start.9 = (bf16[32,4096]{1,0:T(8,128)(2,1)S(1)}, bf16[32,4096]{1,0:T(8,128)(2,1)}, u32[]{:S(2)}) copy-start(bf16[32,4096]{1,0:T(8,128)(2,1)} %get-tuple-element.36.n0) | copy-start | bytes 786436
  6.7 16.8 %copy-start.19 = (bf16[64,4096]{1,0:T(8,128)(2,1)S(1)}, bf16[64,4096]{1,0:T(8,128)(2,1)}, u32[]{:S(2)}) copy-start(bf16[64,4096]{1,0:T(8,128)(2,1)} %get-tuple-element.34) | copy-start | bytes 1572868
  6.7 16.8 %copy-start.18 = (bf16[64,4096]{1,0:T(8,128)(2,1)S(1)}, bf16[64,4096]{1,0:T(8,128)(2,1)}, u32[]{:S(2)}) copy-start(bf16[64,4096]{1,0:T(8,128)(2,1)} %get-tuple-element.35) | copy-start | bytes 1572868
  6.7 17.3 %copy-start.17 = (s32[4,1,256]{2,1,0:T(1,128)S(1)}, s32[4,1,256]{2,1,0:T(1,128)}, u32[]{:S(2)}) copy-start(s32[4,1,256]{2,1,0:T(1,128)} %param.17) | copy-start | bytes 12292
  6.7 45.3 %all-to-all-start = ((bf16[4,192,1024]{2,1,0:T(8,128)(2,1)}), bf16[4,192,1024]{2,1,0:T(8,128)(2,1)}, u32[]{:S(2)}, u32[]{:S(2)}) async-start(bf16[4,192,1024]{2,1,0:T(8,128)(2,1)} %get-tuple-element.37), calls=%async_computation | async-start | bytes 3145728 | tf_op jit(solution)/shard_map/all_to_all | solution.py:58
  11.8 17.0 %collective-permute-start = (bf16[32,4224]{1,0:T(8,128)(2,1)S(1)}, bf16[32,4224]{1,0:T(8,128)(2,1)S(1)}, u32[]{:S(2)}, u32[]{:S(2)}) collective-permute-start(bf16[32,4224]{1,0:T(8,128)(2,1)S(1)} %copy-done.20), channel_id=1, source_target_pairs={{0,248},{1,249},{2,250},{3,251},{4,252},{5,253},{6,254},{7,255},{8... | collective-permute-start | bytes 811016 | tf_op jit(solution)/shard_map/ppermute | solution.py:34
  19.2 28.4 %collective-permute-start.4 = (bf16[32,4224]{1,0:T(8,128)(2,1)S(1)}, bf16[32,4224]{1,0:T(8,128)(2,1)S(1)}, u32[]{:S(2)}, u32[]{:S(2)}) collective-permute-start(bf16[32,4224]{1,0:T(8,128)(2,1)S(1)} %copy-done.20), channel_id=1, source_target_pairs={{0,249},{1,248},{2,251},{3,250},{4,253},{5,252},{6,255},{7,254},{8... | collective-permute-start | bytes 811016 | tf_op jit(solution)/shard_map/ppermute | solution.py:34
  21.7 20.6 %collective-permute-start.3 = (bf16[32,4096]{1,0:T(8,128)(2,1)S(1)}, bf16[32,4096]{1,0:T(8,128)(2,1)S(1)}, u32[]{:S(2)}, u32[]{:S(2)}) collective-permute-start(bf16[32,4096]{1,0:T(8,128)(2,1)S(1)} %copy-done.9), channel_id=1, source_target_pairs={{0,1},{1,0},{2,3},{3,2},{4,5},{5,4},{6,7},{7,6},{8,9},{9,8},{10,11... | collective-permute-start | bytes 786440 | tf_op jit(solution)/shard_map/ppermute | solution.py:34
  23.4 24.2 %collective-permute-start.1 = (bf16[64,4096]{1,0:T(8,128)(2,1)S(1)}, bf16[64,4096]{1,0:T(8,128)(2,1)S(1)}, u32[]{:S(2)}, u32[]{:S(2)}) collective-permute-start(bf16[64,4096]{1,0:T(8,128)(2,1)S(1)} %copy-done.19), channel_id=1, source_target_pairs={{0,8},{1,9},{2,10},{3,11},{4,12},{5,13},{6,14},{7,15},{8,16},{9,17... | collective-permute-start | bytes 1572872 | tf_op jit(solution)/shard_map/ppermute | solution.py:34
  23.5 24.9 %collective-permute-start.2 = (bf16[64,4096]{1,0:T(8,128)(2,1)S(1)}, bf16[64,4096]{1,0:T(8,128)(2,1)}, u32[]{:S(2)}, u32[]{:S(2)}) collective-permute-start(bf16[64,4096]{1,0:T(8,128)(2,1)S(1)} %copy-done.18), channel_id=1, source_target_pairs={{0,248},{1,249},{2,250},{3,251},{4,252},{5,253},{6,254},{7,255},{8... | collective-permute-start | bytes 1572872 | tf_op jit(solution)/shard_map/ppermute | solution.py:34
  28.8 18.8 %copy-start.7 = (bf16[32,4224]{1,0:T(8,128)(2,1)}, bf16[32,4224]{1,0:T(8,128)(2,1)S(1)}, u32[]{:S(2)}) copy-start(bf16[32,4224]{1,0:T(8,128)(2,1)S(1)} %collective-permute-done.n2) | copy-start | bytes 811012
  29.2 22.7 %copy-start.6 = (s32[4,2,4,32]{0,3,2,1:T(8,128)}, s32[4,2,4,32]{0,3,2,1:T(8,128)S(1)}, u32[]{:S(2)}) copy-start(s32[4,2,4,32]{0,3,2,1:T(8,128)S(1)} %copy.20) | copy-start | bytes 12292
  42.3 5.4 %copy-start.10 = (bf16[32,4096]{1,0:T(8,128)(2,1)}, bf16[32,4096]{1,0:T(8,128)(2,1)S(1)}, u32[]{:S(2)}) copy-start(bf16[32,4096]{1,0:T(8,128)(2,1)S(1)} %collective-permute-done.3.n1) | copy-start | bytes 786436
  47.6 0.7 copy-start.8
  48.4 0.9 copy-start
  53.8 19.0 %collective-permute-start.8 = (bf16[4,32,1024]{2,1,0:T(8,128)(2,1)}, bf16[4,32,1024]{2,1,0:T(8,128)(2,1)S(1)}, u32[]{:S(2)}, u32[]{:S(2)}) collective-permute-start(bf16[4,32,1024]{2,1,0:T(8,128)(2,1)} %get-tuple-element.62), channel_id=1, source_target_pairs={{0,241},{1,240},{2,243},{3,242},{4,245},{5,244},{6,247},{7,246},{8... | collective-permute-start | bytes 786440 | tf_op jit(solution)/shard_map/ppermute | solution.py:34
  55.5 25.3 %collective-permute-start.7 = (bf16[4,32,1024]{2,1,0:T(8,128)(2,1)}, bf16[4,32,1024]{2,1,0:T(8,128)(2,1)S(1)}, u32[]{:S(2)}, u32[]{:S(2)}) collective-permute-start(bf16[4,32,1024]{2,1,0:T(8,128)(2,1)} %get-tuple-element.62), channel_id=1, source_target_pairs={{0,240},{1,241},{2,242},{3,243},{4,244},{5,245},{6,246},{7,247},{8... | collective-permute-start | bytes 786440 | tf_op jit(solution)/shard_map/ppermute | solution.py:34
  62.5 24.0 %collective-permute-start.6 = (bf16[4,32,1024]{2,1,0:T(8,128)(2,1)}, bf16[4,32,1024]{2,1,0:T(8,128)(2,1)S(1)}, u32[]{:S(2)}, u32[]{:S(2)}) collective-permute-start(bf16[4,32,1024]{2,1,0:T(8,128)(2,1)} %get-tuple-element.63), channel_id=1, source_target_pairs={{0,249},{1,248},{2,251},{3,250},{4,253},{5,252},{6,255},{7,254},{8... | collective-permute-start | bytes 786440 | tf_op jit(solution)/shard_map/ppermute | solution.py:34
  63.6 22.9 %collective-permute-start.5 = (bf16[4,32,1024]{2,1,0:T(8,128)(2,1)}, bf16[4,32,1024]{2,1,0:T(8,128)(2,1)}, u32[]{:S(2)}, u32[]{:S(2)}) collective-permute-start(bf16[4,32,1024]{2,1,0:T(8,128)(2,1)} %get-tuple-element.63), channel_id=1, source_target_pairs={{0,248},{1,249},{2,250},{3,251},{4,252},{5,253},{6,254},{7,255},{8... | collective-permute-start | bytes 786440 | tf_op jit(solution)/shard_map/ppermute | solution.py:34
  63.6 27.4 %all-to-all-start.1 = ((bf16[4,192,1024]{2,1,0:T(8,128)(2,1)}), bf16[4,192,1024]{2,1,0:T(8,128)(2,1)}, u32[]{:S(2)}, u32[]{:S(2)}) async-start(bf16[4,192,1024]{2,1,0:T(8,128)(2,1)} %shard_map.147), calls=%async_computation.1 | async-start | bytes 3145728 | tf_op jit(solution)/shard_map/all_to_all | solution.py:58
  72.8 13.6 %copy-start.3 = (bf16[4,32,1024]{2,1,0:T(8,128)(2,1)}, bf16[4,32,1024]{2,1,0:T(8,128)(2,1)S(1)}, u32[]{:S(2)}) copy-start(bf16[4,32,1024]{2,1,0:T(8,128)(2,1)S(1)} %collective-permute-done.8.refs_3_) | copy-start | bytes 786436
  80.8 5.6 %copy-start.4 = (bf16[4,32,1024]{2,1,0:T(8,128)(2,1)}, bf16[4,32,1024]{2,1,0:T(8,128)(2,1)S(1)}, u32[]{:S(2)}) copy-start(bf16[4,32,1024]{2,1,0:T(8,128)(2,1)S(1)} %collective-permute-done.7.refs_2_) | copy-start | bytes 786436
  86.4 0.7 copy-start.5
  92.8 31.4 %collective-permute-start.11 = (bf16[4,32,1024]{2,1,0:T(8,128)(2,1)}, bf16[4,32,1024]{2,1,0:T(8,128)(2,1)S(1)}, u32[]{:S(2)}, u32[]{:S(2)}) collective-permute-start(bf16[4,32,1024]{2,1,0:T(8,128)(2,1)} %get-tuple-element.60), channel_id=1, source_target_pairs={{0,249},{1,248},{2,251},{3,250},{4,253},{5,252},{6,255},{7,254},{8... | collective-permute-start | bytes 786440 | tf_op jit(solution)/shard_map/ppermute | solution.py:34
  92.9 31.5 %collective-permute-start.10 = (bf16[4,32,1024]{2,1,0:T(8,128)(2,1)}, bf16[4,32,1024]{2,1,0:T(8,128)(2,1)S(1)}, u32[]{:S(2)}, u32[]{:S(2)}) collective-permute-start(bf16[4,32,1024]{2,1,0:T(8,128)(2,1)} %get-tuple-element.60), channel_id=1, source_target_pairs={{0,248},{1,249},{2,250},{3,251},{4,252},{5,253},{6,254},{7,255},{8... | collective-permute-start | bytes 786440 | tf_op jit(solution)/shard_map/ppermute | solution.py:34
  96.3 28.0 %collective-permute-start.9 = (bf16[4,32,1024]{2,1,0:T(8,128)(2,1)}, bf16[4,32,1024]{2,1,0:T(8,128)(2,1)S(1)}, u32[]{:S(2)}, u32[]{:S(2)}) collective-permute-start(bf16[4,32,1024]{2,1,0:T(8,128)(2,1)} %get-tuple-element.61), channel_id=1, source_target_pairs={{0,1},{1,0},{2,3},{3,2},{4,5},{5,4},{6,7},{7,6},{8,9},{9,8},{10,11... | collective-permute-start | bytes 786440 | tf_op jit(solution)/shard_map/ppermute | solution.py:34
  100.9 20.9 %all-to-all-start.2 = ((bf16[4,1536,128]{2,1,0:T(8,128)(2,1)}), bf16[4,1536,128]{2,1,0:T(8,128)(2,1)}, u32[]{:S(2)}, u32[]{:S(2)}) async-start(bf16[4,1536,128]{2,1,0:T(8,128)(2,1)} %shard_map.149), calls=%async_computation.2 | async-start | bytes 3145728 | tf_op jit(solution)/shard_map/all_to_all | solution.py:58
  124.3 0.8 copy-start.13
  124.3 8.0 %copy-start.11 = (bf16[4,32,1024]{2,1,0:T(8,128)(2,1)}, bf16[4,32,1024]{2,1,0:T(8,128)(2,1)S(1)}, u32[]{:S(2)}) copy-start(bf16[4,32,1024]{2,1,0:T(8,128)(2,1)S(1)} %collective-permute-done.11.refs_3_) | copy-start | bytes 786436
  124.3 0.8 copy-start.12
  125.1 10.6 %all-to-all-start.3 = ((bf16[4,512,128]{2,1,0:T(8,128)(2,1)}), bf16[4,512,128]{2,1,0:T(8,128)(2,1)S(1)}, u32[]{:S(2)}, u32[]{:S(2)}) async-start(bf16[4,512,128]{2,1,0:T(8,128)(2,1)} %shard_map.151), calls=%async_computation.3 | async-start | bytes 1048576 | tf_op jit(solution)/shard_map/all_to_all | solution.py:58
  135.7 0.8 copy-start.2
  139.6 32.0 %collective-permute-start.15 = (bf16[4,32,1024]{2,1,0:T(8,128)(2,1)}, bf16[4,32,1024]{2,1,0:T(8,128)(2,1)S(1)}, u32[]{:S(2)}, u32[]{:S(2)}) collective-permute-start(bf16[4,32,1024]{2,1,0:T(8,128)(2,1)} %get-tuple-element.43), channel_id=1, source_target_pairs={{0,1},{1,0},{2,3},{3,2},{4,5},{5,4},{6,7},{7,6},{8,9},{9,8},{10,11... | collective-permute-start | bytes 786440 | tf_op jit(solution)/shard_map/ppermute | solution.py:34
  145.7 4.4 %copy-start.23 = (bf16[4,32,1024]{2,1,0:T(8,128)(2,1)S(1)}, bf16[4,32,1024]{2,1,0:T(8,128)(2,1)}, u32[]{:S(2)}) copy-start(bf16[4,32,1024]{2,1,0:T(8,128)(2,1)} %get-tuple-element.50) | copy-start | bytes 786436
  145.7 9.5 %copy-start.22 = (bf16[4,32,1024]{2,1,0:T(8,128)(2,1)S(1)}, bf16[4,32,1024]{2,1,0:T(8,128)(2,1)}, u32[]{:S(2)}) copy-start(bf16[4,32,1024]{2,1,0:T(8,128)(2,1)} %get-tuple-element.51) | copy-start | bytes 786436
  145.7 14.2 %all-to-all-start.4 = ((bf16[4,1024,128]{2,1,0:T(8,128)(2,1)}), bf16[4,1024,128]{2,1,0:T(8,128)(2,1)}, u32[]{:S(2)}, u32[]{:S(2)}) async-start(bf16[4,1024,128]{2,1,0:T(8,128)(2,1)} %shard_map.153), calls=%async_computation.4 | async-start | bytes 2097152 | tf_op jit(solution)/shard_map/all_to_all | solution.py:58
  150.1 18.1 %collective-permute-start.16 = (bf16[4,32,1024]{2,1,0:T(8,128)(2,1)S(1)}, bf16[4,32,1024]{2,1,0:T(8,128)(2,1)}, u32[]{:S(2)}, u32[]{:S(2)}) collective-permute-start(bf16[4,32,1024]{2,1,0:T(8,128)(2,1)S(1)} %copy-done.23), channel_id=1, source_target_pairs={{0,248},{1,249},{2,250},{3,251},{4,252},{5,253},{6,254},{7,255},{8... | collective-permute-start | bytes 786440 | tf_op jit(solution)/shard_map/ppermute | solution.py:34
  155.2 16.4 %collective-permute-start.17 = (bf16[4,32,1024]{2,1,0:T(8,128)(2,1)S(1)}, bf16[4,32,1024]{2,1,0:T(8,128)(2,1)}, u32[]{:S(2)}, u32[]{:S(2)}) collective-permute-start(bf16[4,32,1024]{2,1,0:T(8,128)(2,1)S(1)} %copy-done.22), channel_id=1, source_target_pairs={{0,249},{1,248},{2,251},{3,250},{4,253},{5,252},{6,255},{7,254},{8... | collective-permute-start | bytes 786440 | tf_op jit(solution)/shard_map/ppermute | solution.py:34
  162.6 14.1 %all-to-all-start.5 = ((bf16[4,1024,128]{2,1,0:T(8,128)(2,1)}), bf16[4,1024,128]{2,1,0:T(8,128)(2,1)}, u32[]{:S(2)}, u32[]{:S(2)}) async-start(bf16[4,1024,128]{2,1,0:T(8,128)(2,1)} %shard_map.154), calls=%async_computation.5 | async-start | bytes 2097152 | tf_op jit(solution)/shard_map/all_to_all | solution.py:58
  171.6 0.7 copy-start.21
  182.8 4.7 %copy-start.26 = (bf16[4,32,1024]{2,1,0:T(8,128)(2,1)S(1)}, bf16[4,32,1024]{2,1,0:T(8,128)(2,1)}, u32[]{:S(2)}) copy-start(bf16[4,32,1024]{2,1,0:T(8,128)(2,1)} %get-tuple-element.47) | copy-start | bytes 786436
  182.8 22.2 %copy-start.25 = (bf16[4,32,1024]{2,1,0:T(8,128)(2,1)S(1)}, bf16[4,32,1024]{2,1,0:T(8,128)(2,1)}, u32[]{:S(2)}) copy-start(bf16[4,32,1024]{2,1,0:T(8,128)(2,1)} %get-tuple-element.48) | copy-start | bytes 786436
  182.8 23.6 %copy-start.24 = (bf16[4,32,1024]{2,1,0:T(8,128)(2,1)S(1)}, bf16[4,32,1024]{2,1,0:T(8,128)(2,1)}, u32[]{:S(2)}) copy-start(bf16[4,32,1024]{2,1,0:T(8,128)(2,1)} %get-tuple-element.46) | copy-start | bytes 786436
  182.8 53.0 %all-to-all-start.6 = ((bf16[4,320,1024]{2,1,0:T(8,128)(2,1)}), bf16[4,320,1024]{2,1,0:T(8,128)(2,1)}, u32[]{:S(2)}, u32[]{:S(2)}) async-start(bf16[4,320,1024]{2,1,0:T(8,128)(2,1)} %shard_map.159), calls=%async_computation.6 | async-start | bytes 5242880 | tf_op jit(solution)/shard_map/all_to_all | solution.py:58
  187.5 26.6 %collective-permute-start.13 = (bf16[4,32,1024]{2,1,0:T(8,128)(2,1)S(1)}, bf16[4,32,1024]{2,1,0:T(8,128)(2,1)S(1)}, u32[]{:S(2)}, u32[]{:S(2)}) collective-permute-start(bf16[4,32,1024]{2,1,0:T(8,128)(2,1)S(1)} %copy-done.26), channel_id=1, source_target_pairs={{0,248},{1,249},{2,250},{3,251},{4,252},{5,253},{6,254},{7,255},{8... | collective-permute-start | bytes 786440 | tf_op jit(solution)/shard_map/ppermute | solution.py:34
  205.0 27.8 %collective-permute-start.14 = (bf16[4,32,1024]{2,1,0:T(8,128)(2,1)S(1)}, bf16[4,32,1024]{2,1,0:T(8,128)(2,1)S(1)}, u32[]{:S(2)}, u32[]{:S(2)}) collective-permute-start(bf16[4,32,1024]{2,1,0:T(8,128)(2,1)S(1)} %copy-done.25), channel_id=1, source_target_pairs={{0,249},{1,248},{2,251},{3,250},{4,253},{5,252},{6,255},{7,254},{8... | collective-permute-start | bytes 786440 | tf_op jit(solution)/shard_map/ppermute | solution.py:34
  206.5 26.4 %collective-permute-start.12 = (bf16[4,32,1024]{2,1,0:T(8,128)(2,1)S(1)}, bf16[4,32,1024]{2,1,0:T(8,128)(2,1)S(1)}, u32[]{:S(2)}, u32[]{:S(2)}) collective-permute-start(bf16[4,32,1024]{2,1,0:T(8,128)(2,1)S(1)} %copy-done.24), channel_id=1, source_target_pairs={{0,1},{1,0},{2,3},{3,2},{4,5},{5,4},{6,7},{7,6},{8,9},{9,8},{10,11... | collective-permute-start | bytes 786440 | tf_op jit(solution)/shard_map/ppermute | solution.py:34
  214.2 18.6 %copy-start.14 = (bf16[4,32,1024]{2,1,0:T(8,128)(2,1)}, bf16[4,32,1024]{2,1,0:T(8,128)(2,1)S(1)}, u32[]{:S(2)}) copy-start(bf16[4,32,1024]{2,1,0:T(8,128)(2,1)S(1)} %collective-permute-done.13.up_own) | copy-start | bytes 786436
  232.8 0.7 copy-start.15
  232.8 0.8 copy-start.16
  235.8 13.7 %all-to-all-start.7 = ((bf16[4,64,1024]{2,1,0:T(8,128)(2,1)}), bf16[4,64,1024]{2,1,0:T(8,128)(2,1)S(1)}, u32[]{:S(2)}, u32[]{:S(2)}) async-start(bf16[4,64,1024]{2,1,0:T(8,128)(2,1)} %shard_map.156), calls=%async_computation.7 | async-start | bytes 1048576 | tf_op jit(solution)/shard_map/all_to_all | solution.py:58
  249.5 0.8 copy-start.1

commit v2 on v1

--- a/solution.py
+++ b/solution.py
@@ -152,7 +152,9 @@
     for stash, normed in ((down_stash, down_normed), (up_stash, up_normed)):
         x = stash[0].astype(F32)
         normed[:, :WIDTH] = (x * inverse_of(x)).astype(BF16)
-    up_normed[:, WIDTH:] = up_ids[...]
+    ids = [up_ids[job, :, i * HEAD : (i + 1) * HEAD] for job in (1, 3) for i in range(2)]
+    ids.append(jnp.zeros((ROWS - 4, HEAD), jnp.int32))
+    up_normed[:, WIDTH:] = jnp.concatenate(ids, axis=0).astype(F32).astype(BF16)
     columns(cots, 0, HEAD, output_weight[0, 0])
     first = place[0] == 0
     last = place[0] == RANKS - 1
@@ -271,6 +273,11 @@
     rows = jnp.concatenate([flat(piece) for piece in (p0, p1, p2, p3)], axis=0)
     grad = dot(heads(acts), rows, 0, 0).astype(BF16)
     sums[...] = grad.reshape(RING, HEAD, PART)
+
+
+def added_grad_kernel(mixes, output_cols, g0, g1, g2, g3, kept_mixes, sums, *refs):
+    added_kernel(mixes, output_cols, *refs)
+    grad_kernel(g0, g1, g2, g3, kept_mixes, sums)
 
 
 def sum_kernel(own, other, up_own, up_other, sums):
@@ -344,8 +351,6 @@
     narrow, double = out((RING, 2 * TOKENS, HEAD)), out((RING, 4 * TOKENS, HEAD))
     lower, upper, last = (block((RING, 2 * TOKENS, HEAD), 0, i, 0) for i in range(3))
     first = block((RING, PART, HEAD), 0, 0, 0)
-
-    up_ids = jnp.pad(segment_ids[1::2, 0].reshape(4, HEAD), ((0, ROWS - 4), (0, 0))).astype(BF16)
 
     below_sent, above_sent, down_n, up_n, cots = run(
         send_kernel,
@@ -365,7 +370,7 @@
             down_cot,
             up_cot,
             boundary,
-            up_ids,
+            segment_ids,
             (output_weight, block((1, 1, HEAD, WIDTH), 0, 0, 0, 0)),
         ],
     )
@@ -432,23 +437,19 @@
     )
 
     mixes = turned(run(mixed_kernel, [double], [allowed, (values, lower), (values, upper)])[0])
-    added = run(added_kernel, pieces, [(mixes, lower), output_cols])
-    ready = added[1]
-    added = home(added)
-
     tall = out((RING, 2 * HEAD + 2 * ROWS, PART))
     value_part, output_part = (block((RING, HEAD, PART), 0, i, 0) for i in range(2))
     rows_part = block((RING, 2 * ROWS, PART), 0, 4, 0)
     sums = run(grad_kernel, [(tall, value_part)], [*kept, acts], beside=True)[0]
     sums = run(sum_kernel, [(tall, rows_part)], [*normed_grads], filled=sums, beside=True)[0]
-    sums = turned(
-        run(
-            grad_kernel,
-            [(tall, output_part)],
-            [*grads, (after(mixes, ready), upper)],
-            filled=sums,
-        )[0]
-    )
+    sums, *added = run(
+        added_grad_kernel,
+        [(tall, output_part), *pieces],
+        [(mixes, lower), output_cols, *grads, (mixes, upper)],
+        filled=sums,
+    )
+    added = home(added)
+    sums = turned(sums)
     value_grad = run(value_out_kernel, [out((1, WIDTH, HEAD), F32)], [(sums, value_part)])[0]
     output_grad = run(output_out_kernel, [out((1, HEAD, WIDTH), F32)], [(sums, output_part)])[0]
     lower_rows, upper_rows = (block(rows32, i, 0) for i in range(2))

time: 254 us -> 246 us (0.969)
  waiting for transfers between devices: 88.3 us -> 84 us
    ppermute x18, waiting for transfers between devices: 66.7 us -> 63.1 us  [moved(): return lax.ppermute(shard, ('pipe', 'tensor'), pairs)]
    pallas_call x19 -> x18, Pallas kernels: 54.4 us -> 52.6 us  [run(): pl.pallas_call(body, grid=(1,), out_shape=[o for o, _ in outs], in_specs=...]
  transfers between devices with their start and end apart: 26 -> 26, of which waited for: 15 -> 15; matrix products, arithmetic and copies ran while one was open for 0% -> 0% of each run, Pallas kernels for 15% -> 16%
where the time goes in v2:
time: 246 us; the launch traced here: 245 us
  starting transfers between devices  95.7 us (39%)
  waiting for transfers between devices  84 us (34%)
  Pallas kernels  52.6 us (21%)
  local copies, waits for them, and re-layouts  10.9 us (4%)
    ppermute x18, waiting for transfers between devices, moved(): return lax.ppermute(shard, ('pipe', 'tensor'), pairs)  63.1 us
    ppermute x18, starting transfers between devices, moved(): return lax.ppermute(shard, ('pipe', 'tensor'), pairs)  60.8 us
    pallas_call x18, Pallas kernels, run(): pl.pallas_call(body, grid=(1,), out_shape=[o for o, _ in outs], in_specs=...  52.6 us
    all_to_all x8, starting transfers between devices, turned(): lax.all_to_all(blocks, 'tensor', split_axis=0, concat_axis=0, axis_index_...  34.8 us
    all_to_all x8, waiting for transfers between devices, turned(): lax.all_to_all(blocks, 'tensor', split_axis=0, concat_axis=0, axis_index_...  21 us
    unnamed x54, local copies, waits for them, and re-layouts  6.06 us
  transfers between devices with their start and end apart: 26, of which 15 were waited for; matrix products, arithmetic and copies ran while one was open for 0% of the time, Pallas kernels for 16%

profile of v2, /device:TPU:1, one launch (start us, length us, event | category | flops | bytes accessed | tf_op | source)
XLA Modules:
  0.0 244.8 jit_solution(11468684040917175701)
XLA Ops:
  1.2 4.1 %shard_map.145 = (bf16[64,4096]{1,0:T(8,128)(2,1)}, bf16[64,4096]{1,0:T(8,128)(2,1)}, bf16[32,4096]{1,0:T(8,128)(2,1)}, bf16[32,4224]{1,0:T(8,128)(2,1)}, bf16[4,192,1024]{2,1,0:T(8,128)(2,1)}) custom-call(s32[2]{0:T(128)} %pad_add_fusion.place, bf16[1,32,4096]{2,1,0:T(8,128)(2,1)} %down_prev.1, bf16[1,32,4096]{2,1,0:T(8,128)(2,1)} %up_prev.1, ...), custom_call_target="tpu_custom_call" | custom-call | flops 1 | bytes 1 | tf_op jit(solution)/shard_map/pallas_call | solution.py:94
  5.4 5.2 %all-to-all-start = ((bf16[4,192,1024]{2,1,0:T(8,128)(2,1)}), bf16[4,192,1024]{2,1,0:T(8,128)(2,1)}, u32[]{:S(2)}, u32[]{:S(2)}) async-start(bf16[4,192,1024]{2,1,0:T(8,128)(2,1)} %get-tuple-element.36), calls=%async_computation | async-start | bytes 3145728 | tf_op jit(solution)/shard_map/all_to_all | solution.py:58
  10.5 7.4 %collective-permute-start.3 = (bf16[32,4224]{1,0:T(8,128)(2,1)S(1)}, bf16[32,4224]{1,0:T(8,128)(2,1)S(1)}, u32[]{:S(2)}, u32[]{:S(2)}) collective-permute-start(bf16[32,4224]{1,0:T(8,128)(2,1)S(1)} %copy-done.20), channel_id=1, source_target_pairs={{0,248},{1,249},{2,250},{3,251},{4,252},{5,253},{6,254},{7,255},{8... | collective-permute-start | bytes 811016 | tf_op jit(solution)/shard_map/ppermute | solution.py:34
  17.9 2.5 %collective-permute-start.4 = (bf16[32,4224]{1,0:T(8,128)(2,1)S(1)}, bf16[32,4224]{1,0:T(8,128)(2,1)S(1)}, u32[]{:S(2)}, u32[]{:S(2)}) collective-permute-start(bf16[32,4224]{1,0:T(8,128)(2,1)S(1)} %copy-done.20), channel_id=1, source_target_pairs={{0,249},{1,248},{2,251},{3,250},{4,253},{5,252},{6,255},{7,254},{8... | collective-permute-start | bytes 811016 | tf_op jit(solution)/shard_map/ppermute | solution.py:34
  20.4 1.8 collective-permute-start.2
  22.8 5.2 %collective-permute-done.3.n2 = bf16[32,4224]{1,0:T(8,128)(2,1)S(1)} collective-permute-done((bf16[32,4224]{1,0:T(8,128)(2,1)S(1)}, bf16[32,4224]{1,0:T(8,128)(2,1)S(1)}, u32[]{:S(2)}, u32[]{:S(2)}) %collective-permute-start.3) | collective-permute-done | bytes 270368 | tf_op jit(solution)/shard_map/ppermute | solution.py:34
  28.4 0.7 copy.34.ids_row
  29.1 11.9 %collective-permute-done.2.n1 = bf16[32,4096]{1,0:T(8,128)(2,1)S(1)} collective-permute-done((bf16[32,4096]{1,0:T(8,128)(2,1)S(1)}, bf16[32,4096]{1,0:T(8,128)(2,1)S(1)}, u32[]{:S(2)}, u32[]{:S(2)}) %collective-permute-start.2) | collective-permute-done | bytes 262176 | tf_op jit(solution)/shard_map/ppermute | solution.py:34
  41.0 5.3 %collective-permute-done.4.n3 = bf16[32,4224]{1,0:T(8,128)(2,1)S(1)} collective-permute-done((bf16[32,4224]{1,0:T(8,128)(2,1)S(1)}, bf16[32,4224]{1,0:T(8,128)(2,1)S(1)}, u32[]{:S(2)}, u32[]{:S(2)}) %collective-permute-start.4) | collective-permute-done | bytes 270368 | tf_op jit(solution)/shard_map/ppermute | solution.py:34
  46.3 0.7 copy-done.8
  47.0 0.8 copy-done
  47.9 2.7 %shard_map.146 = bf16[4,192,1024]{2,1,0:T(8,128)(2,1)} custom-call(bf16[64,4096]{1,0:T(8,128)(2,1)} %copy-done, bf16[64,4096]{1,0:T(8,128)(2,1)} %collective-permute-done.1.above.up_in.down_grad, bf16[32,4096]{1,0:T(8,128)(2,1)} %get-tuple-element.34.n0, bf16[32,4096]{1,0:T(8,128)(2,1)} %copy-done.10, bf16[32,4224]{1,0:T(8,128)(2,1)} %copy-done.7, ...), custom_call_target="tpu_custom_call" | custom-call | flops 1 | bytes 1 | tf_op jit(solution)/shard_map/pallas_call | solution.py:94
  50.6 1.9 fusion.1
  52.5 1.7 collective-permute-start.8
  54.2 6.9 %collective-permute-start.7 = (bf16[4,32,1024]{2,1,0:T(8,128)(2,1)}, bf16[4,32,1024]{2,1,0:T(8,128)(2,1)S(1)}, u32[]{:S(2)}, u32[]{:S(2)}) collective-permute-start(bf16[4,32,1024]{2,1,0:T(8,128)(2,1)} %get-tuple-element.62), channel_id=1, source_target_pairs={{0,240},{1,241},{2,242},{3,243},{4,244},{5,245},{6,246},{7,247},{8... | collective-permute-start | bytes 786440 | tf_op jit(solution)/shard_map/ppermute | solution.py:34
  61.1 1.1 collective-permute-start.6
  62.2 4.4 %all-to-all-start.1 = ((bf16[4,192,1024]{2,1,0:T(8,128)(2,1)}), bf16[4,192,1024]{2,1,0:T(8,128)(2,1)}, u32[]{:S(2)}, u32[]{:S(2)}) async-start(bf16[4,192,1024]{2,1,0:T(8,128)(2,1)} %shard_map.146), calls=%async_computation.1 | async-start | bytes 3145728 | tf_op jit(solution)/shard_map/all_to_all | solution.py:58
  66.6 2.3 shard_map.148._
  68.8 2.5 %collective-permute-done.8.refs_3_.refs_5_ = bf16[4,32,1024]{2,1,0:T(8,128)(2,1)S(1)} collective-permute-done((bf16[4,32,1024]{2,1,0:T(8,128)(2,1)}, bf16[4,32,1024]{2,1,0:T(8,128)(2,1)S(1)}, u32[]{:S(2)}, u32[]{:S(2)}) %collective-permute-start.8) | collective-permute-done | bytes 262176 | tf_op jit(solution)/shard_map/ppermute | solution.py:34
  71.3 8.2 %collective-permute-done.7.refs_2_.refs_4_ = bf16[4,32,1024]{2,1,0:T(8,128)(2,1)S(1)} collective-permute-done((bf16[4,32,1024]{2,1,0:T(8,128)(2,1)}, bf16[4,32,1024]{2,1,0:T(8,128)(2,1)S(1)}, u32[]{:S(2)}, u32[]{:S(2)}) %collective-permute-start.7) | collective-permute-done | bytes 262176 | tf_op jit(solution)/shard_map/ppermute | solution.py:34
  79.5 5.6 %collective-permute-done.6.refs_1_.refs_3_ = bf16[4,32,1024]{2,1,0:T(8,128)(2,1)S(1)} collective-permute-done((bf16[4,32,1024]{2,1,0:T(8,128)(2,1)}, bf16[4,32,1024]{2,1,0:T(8,128)(2,1)S(1)}, u32[]{:S(2)}, u32[]{:S(2)}) %collective-permute-start.6) | collective-permute-done | bytes 262176 | tf_op jit(solution)/shard_map/ppermute | solution.py:34
  85.1 0.7 copy-done.5
  85.8 3.8 %shard_map.149 = bf16[4,1536,128]{2,1,0:T(8,128)(2,1)} custom-call(bf16[4,1536,128]{2,1,0:T(8,128)(2,1)} %shard_map.148._, bf16[4,32,1024]{2,1,0:T(8,128)(2,1)} %collective-permute-done.5.refs_0_.refs_2_, bf16[4,32,1024]{2,1,0:T(8,128)(2,1)} %copy-done.5, bf16[4,32,1024]{2,1,0:T(8,128)(2,1)} %copy-done.4, ...), custom_call_target="tpu_custom_call", output_to_operand_aliasing={{}: (0, {})} | custom-call | flops 1 | bytes 1 | tf_op jit(solution)/shard_map/pallas_call | solution.py:94
  89.6 1.9 fusion
  91.5 3.4 %collective-permute-start.10 = (bf16[4,32,1024]{2,1,0:T(8,128)(2,1)}, bf16[4,32,1024]{2,1,0:T(8,128)(2,1)S(1)}, u32[]{:S(2)}, u32[]{:S(2)}) collective-permute-start(bf16[4,32,1024]{2,1,0:T(8,128)(2,1)} %get-tuple-element.60), channel_id=1, source_target_pairs={{0,248},{1,249},{2,250},{3,251},{4,252},{5,253},{6,254},{7,255},{8... | collective-permute-start | bytes 786440 | tf_op jit(solution)/shard_map/ppermute | solution.py:34
  94.9 4.6 %collective-permute-start.9 = (bf16[4,32,1024]{2,1,0:T(8,128)(2,1)}, bf16[4,32,1024]{2,1,0:T(8,128)(2,1)S(1)}, u32[]{:S(2)}, u32[]{:S(2)}) collective-permute-start(bf16[4,32,1024]{2,1,0:T(8,128)(2,1)} %get-tuple-element.61), channel_id=1, source_target_pairs={{0,1},{1,0},{2,3},{3,2},{4,5},{5,4},{6,7},{7,6},{8,9},{9,8},{10,11... | collective-permute-start | bytes 786440 | tf_op jit(solution)/shard_map/ppermute | solution.py:34
  99.5 4.4 %all-to-all-start.2 = ((bf16[4,1536,128]{2,1,0:T(8,128)(2,1)}), bf16[4,1536,128]{2,1,0:T(8,128)(2,1)}, u32[]{:S(2)}, u32[]{:S(2)}) async-start(bf16[4,1536,128]{2,1,0:T(8,128)(2,1)} %shard_map.149), calls=%async_computation.2 | async-start | bytes 3145728 | tf_op jit(solution)/shard_map/all_to_all | solution.py:58
  103.9 2.1 shard_map.147
  106.0 14.5 %all-to-all-done.2.sums.value_cols.refs_4_ = bf16[4,1536,128]{2,1,0:T(8,128)(2,1)} async-done(((bf16[4,1536,128]{2,1,0:T(8,128)(2,1)}), bf16[4,1536,128]{2,1,0:T(8,128)(2,1)}, u32[]{:S(2)}, u32[]{:S(2)}) %all-to-all-start.2) | async-done | bytes 1572896 | tf_op jit(solution)/shard_map/all_to_all | solution.py:58
  120.5 2.4 shard_map.150
  123.0 0.8 copy-done.13
  123.7 3.6 %all-to-all-start.3 = ((bf16[4,512,128]{2,1,0:T(8,128)(2,1)}), bf16[4,512,128]{2,1,0:T(8,128)(2,1)S(1)}, u32[]{:S(2)}, u32[]{:S(2)}) async-start(bf16[4,512,128]{2,1,0:T(8,128)(2,1)} %shard_map.150), calls=%async_computation.3 | async-start | bytes 1048576 | tf_op jit(solution)/shard_map/all_to_all | solution.py:58
  127.3 3.6 %shard_map.154._ = bf16[4,1024,128]{2,1,0:T(8,128)(2,1)} custom-call(bf16[4,192,1024]{2,1,0:T(8,128)(2,1)} %all-to-all-done.1.p0.p1.p2.p3.x0.x1.x2.x3.refs_0_, bf16[4,192,1024]{2,1,0:T(8,128)(2,1)} %all-to-all-done.1.p0.p1.p2.p3.x0.x1.x2.x3.refs_0_, bf16[4,192,1024]{2,1,0:T(8,128)(2,1)} %all-to-all-done.1.p0.p1.p2.p3.x0.x1.x2.x3.refs_0_, ...), custom_call_target="tpu_custom_call" | custom-call | flops 1 | bytes 1 | tf_op jit(solution)/shard_map/pallas_call | solution.py:94
  130.9 3.3 %all-to-all-done.3.acts = bf16[4,512,128]{2,1,0:T(8,128)(2,1)S(1)} async-done(((bf16[4,512,128]{2,1,0:T(8,128)(2,1)}), bf16[4,512,128]{2,1,0:T(8,128)(2,1)S(1)}, u32[]{:S(2)}, u32[]{:S(2)}) %all-to-all-start.3) | async-done | bytes 524320 | tf_op jit(solution)/shard_map/all_to_all | solution.py:58
  134.3 0.8 copy-done.2
  135.1 3.1 %shard_map.152 = (f32[4,32,1024]{2,1,0:T(8,128)}, bf16[4,32,1024]{2,1,0:T(8,128)(2,1)}, bf16[4,32,1024]{2,1,0:T(8,128)(2,1)}, bf16[4,32,1024]{2,1,0:T(8,128)(2,1)}) custom-call(bf16[4,512,128]{2,1,0:T(8,128)(2,1)} %copy-done.2, bf16[4,1536,128]{2,1,0:T(8,128)(2,1)} %all-to-all-done.2.sums.value_cols.refs_4_), custom_call_target="tpu_custom_call" | custom-call | flops 1 | bytes 1 | tf_op jit(solution)/shard_map/pallas_call | solution.py:94
  138.2 2.6 %collective-permute-start.12 = (bf16[4,32,1024]{2,1,0:T(8,128)(2,1)}, bf16[4,32,1024]{2,1,0:T(8,128)(2,1)S(1)}, u32[]{:S(2)}, u32[]{:S(2)}) collective-permute-start(bf16[4,32,1024]{2,1,0:T(8,128)(2,1)} %get-tuple-element.44), channel_id=1, source_target_pairs={{0,1},{1,0},{2,3},{3,2},{4,5},{5,4},{6,7},{7,6},{8,9},{9,8},{10,11... | collective-permute-start | bytes 786440 | tf_op jit(solution)/shard_map/ppermute | solution.py:34
  140.8 3.6 %shard_map.155 = bf16[4,1024,128]{2,1,0:T(8,128)(2,1)} custom-call(bf16[4,1024,128]{2,1,0:T(8,128)(2,1)} %shard_map.154._, bf16[4,192,1024]{2,1,0:T(8,128)(2,1)} %all-to-all-done.1.p0.p1.p2.p3.x0.x1.x2.x3.refs_0_, bf16[4,32,1024]{2,1,0:T(8,128)(2,1)} %copy-done.13, bf16[4,32,1024]{2,1,0:T(8,128)(2,1)} %copy-done.12, ...), custom_call_target="tpu_custom_call", output_to_operand_aliasing={{}: (0, {})} | custom-call | flops 1 | bytes 1 | tf_op jit(solution)/shard_map/pallas_call | solution.py:94
  144.4 4.4 %all-to-all-start.4 = ((bf16[4,1024,128]{2,1,0:T(8,128)(2,1)}), bf16[4,1024,128]{2,1,0:T(8,128)(2,1)}, u32[]{:S(2)}, u32[]{:S(2)}) async-start(bf16[4,1024,128]{2,1,0:T(8,128)(2,1)} %shard_map.155), calls=%async_computation.4 | async-start | bytes 2097152 | tf_op jit(solution)/shard_map/all_to_all | solution.py:58
  148.8 5.0 %collective-permute-start.13 = (bf16[4,32,1024]{2,1,0:T(8,128)(2,1)S(1)}, bf16[4,32,1024]{2,1,0:T(8,128)(2,1)}, u32[]{:S(2)}, u32[]{:S(2)}) collective-permute-start(bf16[4,32,1024]{2,1,0:T(8,128)(2,1)S(1)} %copy-done.23), channel_id=1, source_target_pairs={{0,248},{1,249},{2,250},{3,251},{4,252},{5,253},{6,254},{7,255},{8... | collective-permute-start | bytes 786440 | tf_op jit(solution)/shard_map/ppermute | solution.py:34
  153.8 1.4 collective-permute-start.14
  155.2 3.1 %shard_map.151._ = bf16[4,320,1024]{2,1,0:T(8,128)(2,1)} custom-call(bf16[4,192,1024]{2,1,0:T(8,128)(2,1)} %all-to-all-done.1.p0.p1.p2.p3.x0.x1.x2.x3.refs_0_, bf16[4,192,1024]{2,1,0:T(8,128)(2,1)} %all-to-all-done.1.p0.p1.p2.p3.x0.x1.x2.x3.refs_0_, bf16[4,192,1024]{2,1,0:T(8,128)(2,1)} %all-to-all-done.1.p0.p1.p2.p3.x0.x1.x2.x3.refs_0_, ...), custom_call_target="tpu_custom_call" | custom-call | flops 99999997952 | bytes 1 | tf_op jit(solution)/shard_map/pallas_call | solution.py:94
  158.6 2.7 %shard_map.156 = bf16[4,1024,128]{2,1,0:T(8,128)(2,1)} custom-call(bf16[4,256,256]{2,1,0:T(8,128)(2,1)} %get-tuple-element.38.allowed, bf16[4,1024,128]{2,1,0:T(8,128)(2,1)} %all-to-all-done.4.first.second, bf16[4,1024,128]{2,1,0:T(8,128)(2,1)} %all-to-all-done.4.first.second), custom_call_target="tpu_custom_call" | custom-call | flops 1 | bytes 1 | tf_op jit(solution)/shard_map/pallas_call | solution.py:94
  161.3 4.3 %all-to-all-start.5 = ((bf16[4,1024,128]{2,1,0:T(8,128)(2,1)}), bf16[4,1024,128]{2,1,0:T(8,128)(2,1)}, u32[]{:S(2)}, u32[]{:S(2)}) async-start(bf16[4,1024,128]{2,1,0:T(8,128)(2,1)} %shard_map.156), calls=%async_computation.5 | async-start | bytes 2097152 | tf_op jit(solution)/shard_map/all_to_all | solution.py:58
  165.5 1.8 collective-permute-done.13.refs_2_
  167.4 2.9 %collective-permute-done.14.refs_3_ = bf16[4,32,1024]{2,1,0:T(8,128)(2,1)} collective-permute-done((bf16[4,32,1024]{2,1,0:T(8,128)(2,1)S(1)}, bf16[4,32,1024]{2,1,0:T(8,128)(2,1)}, u32[]{:S(2)}, u32[]{:S(2)}) %collective-permute-start.14) | collective-permute-done | bytes 262176 | tf_op jit(solution)/shard_map/ppermute | solution.py:34
  170.2 0.7 copy-done.21
  170.9 2.2 shard_map.153._
  173.1 2.2 all-to-all-done.5.refs_0_.refs_6_
  175.3 4.5 %shard_map.157 = (bf16[4,320,1024]{2,1,0:T(8,128)(2,1)}, f32[4,32,1024]{2,1,0:T(8,128)}, bf16[4,32,1024]{2,1,0:T(8,128)(2,1)}, bf16[4,32,1024]{2,1,0:T(8,128)(2,1)}, bf16[4,32,1024]{2,1,0:T(8,128)(2,1)}) custom-call(bf16[4,320,1024]{2,1,0:T(8,128)(2,1)} %shard_map.153._, ...), custom_call_target="tpu_custom_call", output_to_operand_aliasing={{0}: (0, {})} | custom-call | flops 1 | bytes 1 | tf_op jit(solution)/shard_map/pallas_call | solution.py:94
  179.8 4.7 %all-to-all-start.6 = ((bf16[4,320,1024]{2,1,0:T(8,128)(2,1)}), bf16[4,320,1024]{2,1,0:T(8,128)(2,1)}, u32[]{:S(2)}, u32[]{:S(2)}) async-start(bf16[4,320,1024]{2,1,0:T(8,128)(2,1)} %get-tuple-element.52), calls=%async_computation.6 | async-start | bytes 5242880 | tf_op jit(solution)/shard_map/all_to_all | solution.py:58
  184.5 2.9 %collective-permute-start.15 = (bf16[4,32,1024]{2,1,0:T(8,128)(2,1)S(1)}, bf16[4,32,1024]{2,1,0:T(8,128)(2,1)S(1)}, u32[]{:S(2)}, u32[]{:S(2)}) collective-permute-start(bf16[4,32,1024]{2,1,0:T(8,128)(2,1)S(1)} %copy-done.26), channel_id=1, source_target_pairs={{0,1},{1,0},{2,3},{3,2},{4,5},{5,4},{6,7},{7,6},{8,9},{9,8},{10,11... | collective-permute-start | bytes 786440 | tf_op jit(solution)/shard_map/ppermute | solution.py:34
  187.4 19.1 %collective-permute-start.16 = (bf16[4,32,1024]{2,1,0:T(8,128)(2,1)S(1)}, bf16[4,32,1024]{2,1,0:T(8,128)(2,1)S(1)}, u32[]{:S(2)}, u32[]{:S(2)}) collective-permute-start(bf16[4,32,1024]{2,1,0:T(8,128)(2,1)S(1)} %copy-done.25), channel_id=1, source_target_pairs={{0,248},{1,249},{2,250},{3,251},{4,252},{5,253},{6,254},{7,255},{8... | collective-permute-start | bytes 786440 | tf_op jit(solution)/shard_map/ppermute | solution.py:34
  206.5 15.1 %collective-permute-done.16.up_own = bf16[4,32,1024]{2,1,0:T(8,128)(2,1)S(1)} collective-permute-done((bf16[4,32,1024]{2,1,0:T(8,128)(2,1)S(1)}, bf16[4,32,1024]{2,1,0:T(8,128)(2,1)S(1)}, u32[]{:S(2)}, u32[]{:S(2)}) %collective-permute-start.16) | collective-permute-done | bytes 262176 | tf_op jit(solution)/shard_map/ppermute | solution.py:34
  221.6 4.5 %collective-permute-done.17.up_other = bf16[4,32,1024]{2,1,0:T(8,128)(2,1)S(1)} collective-permute-done((bf16[4,32,1024]{2,1,0:T(8,128)(2,1)S(1)}, bf16[4,32,1024]{2,1,0:T(8,128)(2,1)S(1)}, u32[]{:S(2)}, u32[]{:S(2)}) %collective-permute-start.17) | collective-permute-done | bytes 262176 | tf_op jit(solution)/shard_map/ppermute | solution.py:34
  226.2 0.7 copy-done.16
  226.8 2.2 shard_map.158
  229.0 4.0 %all-to-all-start.7 = ((bf16[4,64,1024]{2,1,0:T(8,128)(2,1)}), bf16[4,64,1024]{2,1,0:T(8,128)(2,1)S(1)}, u32[]{:S(2)}, u32[]{:S(2)}) async-start(bf16[4,64,1024]{2,1,0:T(8,128)(2,1)} %shard_map.158), calls=%async_computation.7 | async-start | bytes 1048576 | tf_op jit(solution)/shard_map/all_to_all | solution.py:58
  233.0 2.7 %shard_map.160 = (bf16[1,32,4096]{2,1,0:T(8,128)(2,1)}, bf16[1,32,4096]{2,1,0:T(8,128)(2,1)}) custom-call(bf16[4,320,1024]{2,1,0:T(8,128)(2,1)} %all-to-all-done.6.got, bf16[64,4096]{1,0:T(8,128)(2,1)} %collective-permute-done.1.above.up_in.down_grad, bf16[64,4096]{1,0:T(8,128)(2,1)} %copy-done, bf16[1,32,4096]{2,1,0:T(8,128)(2,1)} %down_stash.3, ...), custom_call_target="tpu_custom_call" | custom-call | flops 1 | bytes 1 | tf_op jit(solution)/shard_map/pallas_call | solution.py:94
  235.7 2.7 %shard_map.162 = f32[1,128,4096]{2,1,0:T(8,128)} custom-call(bf16[4,320,1024]{2,1,0:T(8,128)(2,1)} %all-to-all-done.6.got), custom_call_target="tpu_custom_call" | custom-call | flops 1 | bytes 1 | tf_op jit(solution)/shard_map/pallas_call | solution.py:94
  238.4 2.9 %shard_map.161 = f32[1,4096,128]{2,1,0:T(8,128)} custom-call(bf16[4,320,1024]{2,1,0:T(8,128)(2,1)} %all-to-all-done.6.got), custom_call_target="tpu_custom_call" | custom-call | flops 1 | bytes 1 | tf_op jit(solution)/shard_map/pallas_call | solution.py:94
  241.3 0.6 all-to-all-done.7.got
  241.9 0.8 copy-done.1
  242.7 2.0 shard_map.159
  (78 shorter events, 2.0 us)
Async XLA Ops:
  5.3 5.2 %copy-start.20 = (bf16[32,4224]{1,0:T(8,128)(2,1)S(1)}, bf16[32,4224]{1,0:T(8,128)(2,1)}, u32[]{:S(2)}) copy-start(bf16[32,4224]{1,0:T(8,128)(2,1)} %get-tuple-element.35) | copy-start | bytes 811012
  5.3 15.0 %copy-start.9 = (bf16[32,4096]{1,0:T(8,128)(2,1)S(1)}, bf16[32,4096]{1,0:T(8,128)(2,1)}, u32[]{:S(2)}) copy-start(bf16[32,4096]{1,0:T(8,128)(2,1)} %get-tuple-element.34.n0) | copy-start | bytes 786436
  5.3 16.8 %copy-start.19 = (bf16[64,4096]{1,0:T(8,128)(2,1)S(1)}, bf16[64,4096]{1,0:T(8,128)(2,1)}, u32[]{:S(2)}) copy-start(bf16[64,4096]{1,0:T(8,128)(2,1)} %get-tuple-element.32) | copy-start | bytes 1572868
  5.3 16.8 %copy-start.18 = (bf16[64,4096]{1,0:T(8,128)(2,1)S(1)}, bf16[64,4096]{1,0:T(8,128)(2,1)}, u32[]{:S(2)}) copy-start(bf16[64,4096]{1,0:T(8,128)(2,1)} %get-tuple-element.33) | copy-start | bytes 1572868
  5.4 17.3 %copy-start.17 = (s32[4,1,256]{2,1,0:T(1,128)S(1)}, s32[4,1,256]{2,1,0:T(1,128)}, u32[]{:S(2)}) copy-start(s32[4,1,256]{2,1,0:T(1,128)} %up_ids.1) | copy-start | bytes 12292
  5.4 45.3 %all-to-all-start = ((bf16[4,192,1024]{2,1,0:T(8,128)(2,1)}), bf16[4,192,1024]{2,1,0:T(8,128)(2,1)}, u32[]{:S(2)}, u32[]{:S(2)}) async-start(bf16[4,192,1024]{2,1,0:T(8,128)(2,1)} %get-tuple-element.36), calls=%async_computation | async-start | bytes 3145728 | tf_op jit(solution)/shard_map/all_to_all | solution.py:58
  10.5 17.6 %collective-permute-start.3 = (bf16[32,4224]{1,0:T(8,128)(2,1)S(1)}, bf16[32,4224]{1,0:T(8,128)(2,1)S(1)}, u32[]{:S(2)}, u32[]{:S(2)}) collective-permute-start(bf16[32,4224]{1,0:T(8,128)(2,1)S(1)} %copy-done.20), channel_id=1, source_target_pairs={{0,248},{1,249},{2,250},{3,251},{4,252},{5,253},{6,254},{7,255},{8... | collective-permute-start | bytes 811016 | tf_op jit(solution)/shard_map/ppermute | solution.py:34
  17.9 28.4 %collective-permute-start.4 = (bf16[32,4224]{1,0:T(8,128)(2,1)S(1)}, bf16[32,4224]{1,0:T(8,128)(2,1)S(1)}, u32[]{:S(2)}, u32[]{:S(2)}) collective-permute-start(bf16[32,4224]{1,0:T(8,128)(2,1)S(1)} %copy-done.20), channel_id=1, source_target_pairs={{0,249},{1,248},{2,251},{3,250},{4,253},{5,252},{6,255},{7,254},{8... | collective-permute-start | bytes 811016 | tf_op jit(solution)/shard_map/ppermute | solution.py:34
  20.4 20.6 %collective-permute-start.2 = (bf16[32,4096]{1,0:T(8,128)(2,1)S(1)}, bf16[32,4096]{1,0:T(8,128)(2,1)S(1)}, u32[]{:S(2)}, u32[]{:S(2)}) collective-permute-start(bf16[32,4096]{1,0:T(8,128)(2,1)S(1)} %copy-done.9), channel_id=1, source_target_pairs={{0,1},{1,0},{2,3},{3,2},{4,5},{5,4},{6,7},{7,6},{8,9},{9,8},{10,11... | collective-permute-start | bytes 786440 | tf_op jit(solution)/shard_map/ppermute | solution.py:34
  22.1 24.2 %collective-permute-start = (bf16[64,4096]{1,0:T(8,128)(2,1)S(1)}, bf16[64,4096]{1,0:T(8,128)(2,1)S(1)}, u32[]{:S(2)}, u32[]{:S(2)}) collective-permute-start(bf16[64,4096]{1,0:T(8,128)(2,1)S(1)} %copy-done.19), channel_id=1, source_target_pairs={{0,8},{1,9},{2,10},{3,11},{4,12},{5,13},{6,14},{7,15},{8,16},{9,17... | collective-permute-start | bytes 1572872 | tf_op jit(solution)/shard_map/ppermute | solution.py:34
  22.1 24.9 %collective-permute-start.1 = (bf16[64,4096]{1,0:T(8,128)(2,1)S(1)}, bf16[64,4096]{1,0:T(8,128)(2,1)}, u32[]{:S(2)}, u32[]{:S(2)}) collective-permute-start(bf16[64,4096]{1,0:T(8,128)(2,1)S(1)} %copy-done.18), channel_id=1, source_target_pairs={{0,248},{1,249},{2,250},{3,251},{4,252},{5,253},{6,254},{7,255},{8... | collective-permute-start | bytes 1572872 | tf_op jit(solution)/shard_map/ppermute | solution.py:34
  28.1 18.2 %copy-start.7 = (bf16[32,4224]{1,0:T(8,128)(2,1)}, bf16[32,4224]{1,0:T(8,128)(2,1)S(1)}, u32[]{:S(2)}) copy-start(bf16[32,4224]{1,0:T(8,128)(2,1)S(1)} %collective-permute-done.3.n2) | copy-start | bytes 811012
  28.4 22.2 %copy-start.6 = (s32[4,2,4,32]{0,3,2,1:T(8,128)}, s32[4,2,4,32]{0,3,2,1:T(8,128)S(1)}, u32[]{:S(2)}) copy-start(s32[4,2,4,32]{0,3,2,1:T(8,128)S(1)} %copy.33) | copy-start | bytes 12292
  41.0 5.3 %copy-start.10 = (bf16[32,4096]{1,0:T(8,128)(2,1)}, bf16[32,4096]{1,0:T(8,128)(2,1)S(1)}, u32[]{:S(2)}) copy-start(bf16[32,4096]{1,0:T(8,128)(2,1)S(1)} %collective-permute-done.2.n1) | copy-start | bytes 786436
  46.3 0.7 copy-start.8
  47.0 0.9 copy-start
  52.5 18.8 %collective-permute-start.8 = (bf16[4,32,1024]{2,1,0:T(8,128)(2,1)}, bf16[4,32,1024]{2,1,0:T(8,128)(2,1)S(1)}, u32[]{:S(2)}, u32[]{:S(2)}) collective-permute-start(bf16[4,32,1024]{2,1,0:T(8,128)(2,1)} %get-tuple-element.62), channel_id=1, source_target_pairs={{0,241},{1,240},{2,243},{3,242},{4,245},{5,244},{6,247},{7,246},{8... | collective-permute-start | bytes 786440 | tf_op jit(solution)/shard_map/ppermute | solution.py:34
  54.2 25.3 %collective-permute-start.7 = (bf16[4,32,1024]{2,1,0:T(8,128)(2,1)}, bf16[4,32,1024]{2,1,0:T(8,128)(2,1)S(1)}, u32[]{:S(2)}, u32[]{:S(2)}) collective-permute-start(bf16[4,32,1024]{2,1,0:T(8,128)(2,1)} %get-tuple-element.62), channel_id=1, source_target_pairs={{0,240},{1,241},{2,242},{3,243},{4,244},{5,245},{6,246},{7,247},{8... | collective-permute-start | bytes 786440 | tf_op jit(solution)/shard_map/ppermute | solution.py:34
  61.1 24.0 %collective-permute-start.6 = (bf16[4,32,1024]{2,1,0:T(8,128)(2,1)}, bf16[4,32,1024]{2,1,0:T(8,128)(2,1)S(1)}, u32[]{:S(2)}, u32[]{:S(2)}) collective-permute-start(bf16[4,32,1024]{2,1,0:T(8,128)(2,1)} %get-tuple-element.63), channel_id=1, source_target_pairs={{0,249},{1,248},{2,251},{3,250},{4,253},{5,252},{6,255},{7,254},{8... | collective-permute-start | bytes 786440 | tf_op jit(solution)/shard_map/ppermute | solution.py:34
  62.2 22.9 %collective-permute-start.5 = (bf16[4,32,1024]{2,1,0:T(8,128)(2,1)}, bf16[4,32,1024]{2,1,0:T(8,128)(2,1)}, u32[]{:S(2)}, u32[]{:S(2)}) collective-permute-start(bf16[4,32,1024]{2,1,0:T(8,128)(2,1)} %get-tuple-element.63), channel_id=1, source_target_pairs={{0,248},{1,249},{2,250},{3,251},{4,252},{5,253},{6,254},{7,255},{8... | collective-permute-start | bytes 786440 | tf_op jit(solution)/shard_map/ppermute | solution.py:34
  62.2 27.5 %all-to-all-start.1 = ((bf16[4,192,1024]{2,1,0:T(8,128)(2,1)}), bf16[4,192,1024]{2,1,0:T(8,128)(2,1)}, u32[]{:S(2)}, u32[]{:S(2)}) async-start(bf16[4,192,1024]{2,1,0:T(8,128)(2,1)} %shard_map.146), calls=%async_computation.1 | async-start | bytes 3145728 | tf_op jit(solution)/shard_map/all_to_all | solution.py:58
  71.3 13.8 %copy-start.3 = (bf16[4,32,1024]{2,1,0:T(8,128)(2,1)}, bf16[4,32,1024]{2,1,0:T(8,128)(2,1)S(1)}, u32[]{:S(2)}) copy-start(bf16[4,32,1024]{2,1,0:T(8,128)(2,1)S(1)} %collective-permute-done.8.refs_3_.refs_5_) | copy-start | bytes 786436
  79.5 5.6 %copy-start.4 = (bf16[4,32,1024]{2,1,0:T(8,128)(2,1)}, bf16[4,32,1024]{2,1,0:T(8,128)(2,1)S(1)}, u32[]{:S(2)}) copy-start(bf16[4,32,1024]{2,1,0:T(8,128)(2,1)S(1)} %collective-permute-done.7.refs_2_.refs_4_) | copy-start | bytes 786436
  85.1 0.7 copy-start.5
  91.5 31.4 %collective-permute-start.11 = (bf16[4,32,1024]{2,1,0:T(8,128)(2,1)}, bf16[4,32,1024]{2,1,0:T(8,128)(2,1)S(1)}, u32[]{:S(2)}, u32[]{:S(2)}) collective-permute-start(bf16[4,32,1024]{2,1,0:T(8,128)(2,1)} %get-tuple-element.60), channel_id=1, source_target_pairs={{0,249},{1,248},{2,251},{3,250},{4,253},{5,252},{6,255},{7,254},{8... | collective-permute-start | bytes 786440 | tf_op jit(solution)/shard_map/ppermute | solution.py:34
  91.5 31.4 %collective-permute-start.10 = (bf16[4,32,1024]{2,1,0:T(8,128)(2,1)}, bf16[4,32,1024]{2,1,0:T(8,128)(2,1)S(1)}, u32[]{:S(2)}, u32[]{:S(2)}) collective-permute-start(bf16[4,32,1024]{2,1,0:T(8,128)(2,1)} %get-tuple-element.60), channel_id=1, source_target_pairs={{0,248},{1,249},{2,250},{3,251},{4,252},{5,253},{6,254},{7,255},{8... | collective-permute-start | bytes 786440 | tf_op jit(solution)/shard_map/ppermute | solution.py:34
  94.9 28.0 %collective-permute-start.9 = (bf16[4,32,1024]{2,1,0:T(8,128)(2,1)}, bf16[4,32,1024]{2,1,0:T(8,128)(2,1)S(1)}, u32[]{:S(2)}, u32[]{:S(2)}) collective-permute-start(bf16[4,32,1024]{2,1,0:T(8,128)(2,1)} %get-tuple-element.61), channel_id=1, source_target_pairs={{0,1},{1,0},{2,3},{3,2},{4,5},{5,4},{6,7},{7,6},{8,9},{9,8},{10,11... | collective-permute-start | bytes 786440 | tf_op jit(solution)/shard_map/ppermute | solution.py:34
  99.5 20.9 %all-to-all-start.2 = ((bf16[4,1536,128]{2,1,0:T(8,128)(2,1)}), bf16[4,1536,128]{2,1,0:T(8,128)(2,1)}, u32[]{:S(2)}, u32[]{:S(2)}) async-start(bf16[4,1536,128]{2,1,0:T(8,128)(2,1)} %shard_map.149), calls=%async_computation.2 | async-start | bytes 3145728 | tf_op jit(solution)/shard_map/all_to_all | solution.py:58
  122.9 0.8 copy-start.13
  122.9 8.0 %copy-start.11 = (bf16[4,32,1024]{2,1,0:T(8,128)(2,1)}, bf16[4,32,1024]{2,1,0:T(8,128)(2,1)S(1)}, u32[]{:S(2)}) copy-start(bf16[4,32,1024]{2,1,0:T(8,128)(2,1)S(1)} %collective-permute-done.11.refs_3_) | copy-start | bytes 786436
  123.0 0.8 copy-start.12
  123.7 10.6 %all-to-all-start.3 = ((bf16[4,512,128]{2,1,0:T(8,128)(2,1)}), bf16[4,512,128]{2,1,0:T(8,128)(2,1)S(1)}, u32[]{:S(2)}, u32[]{:S(2)}) async-start(bf16[4,512,128]{2,1,0:T(8,128)(2,1)} %shard_map.150), calls=%async_computation.3 | async-start | bytes 1048576 | tf_op jit(solution)/shard_map/all_to_all | solution.py:58
  134.3 0.8 copy-start.2
  138.2 32.1 %collective-permute-start.12 = (bf16[4,32,1024]{2,1,0:T(8,128)(2,1)}, bf16[4,32,1024]{2,1,0:T(8,128)(2,1)S(1)}, u32[]{:S(2)}, u32[]{:S(2)}) collective-permute-start(bf16[4,32,1024]{2,1,0:T(8,128)(2,1)} %get-tuple-element.44), channel_id=1, source_target_pairs={{0,1},{1,0},{2,3},{3,2},{4,5},{5,4},{6,7},{7,6},{8,9},{9,8},{10,11... | collective-permute-start | bytes 786440 | tf_op jit(solution)/shard_map/ppermute | solution.py:34
  144.4 4.4 %copy-start.23 = (bf16[4,32,1024]{2,1,0:T(8,128)(2,1)S(1)}, bf16[4,32,1024]{2,1,0:T(8,128)(2,1)}, u32[]{:S(2)}) copy-start(bf16[4,32,1024]{2,1,0:T(8,128)(2,1)} %get-tuple-element.45) | copy-start | bytes 786436
  144.4 9.5 %copy-start.22 = (bf16[4,32,1024]{2,1,0:T(8,128)(2,1)S(1)}, bf16[4,32,1024]{2,1,0:T(8,128)(2,1)}, u32[]{:S(2)}) copy-start(bf16[4,32,1024]{2,1,0:T(8,128)(2,1)} %get-tuple-element.46) | copy-start | bytes 786436
  144.4 14.2 %all-to-all-start.4 = ((bf16[4,1024,128]{2,1,0:T(8,128)(2,1)}), bf16[4,1024,128]{2,1,0:T(8,128)(2,1)}, u32[]{:S(2)}, u32[]{:S(2)}) async-start(bf16[4,1024,128]{2,1,0:T(8,128)(2,1)} %shard_map.155), calls=%async_computation.4 | async-start | bytes 2097152 | tf_op jit(solution)/shard_map/all_to_all | solution.py:58
  148.8 18.6 %collective-permute-start.13 = (bf16[4,32,1024]{2,1,0:T(8,128)(2,1)S(1)}, bf16[4,32,1024]{2,1,0:T(8,128)(2,1)}, u32[]{:S(2)}, u32[]{:S(2)}) collective-permute-start(bf16[4,32,1024]{2,1,0:T(8,128)(2,1)S(1)} %copy-done.23), channel_id=1, source_target_pairs={{0,248},{1,249},{2,250},{3,251},{4,252},{5,253},{6,254},{7,255},{8... | collective-permute-start | bytes 786440 | tf_op jit(solution)/shard_map/ppermute | solution.py:34
  153.8 16.4 %collective-permute-start.14 = (bf16[4,32,1024]{2,1,0:T(8,128)(2,1)S(1)}, bf16[4,32,1024]{2,1,0:T(8,128)(2,1)}, u32[]{:S(2)}, u32[]{:S(2)}) collective-permute-start(bf16[4,32,1024]{2,1,0:T(8,128)(2,1)S(1)} %copy-done.22), channel_id=1, source_target_pairs={{0,249},{1,248},{2,251},{3,250},{4,253},{5,252},{6,255},{7,254},{8... | collective-permute-start | bytes 786440 | tf_op jit(solution)/shard_map/ppermute | solution.py:34
  161.3 14.1 %all-to-all-start.5 = ((bf16[4,1024,128]{2,1,0:T(8,128)(2,1)}), bf16[4,1024,128]{2,1,0:T(8,128)(2,1)}, u32[]{:S(2)}, u32[]{:S(2)}) async-start(bf16[4,1024,128]{2,1,0:T(8,128)(2,1)} %shard_map.156), calls=%async_computation.5 | async-start | bytes 2097152 | tf_op jit(solution)/shard_map/all_to_all | solution.py:58
  170.2 0.7 copy-start.21
  179.8 4.7 %copy-start.26 = (bf16[4,32,1024]{2,1,0:T(8,128)(2,1)S(1)}, bf16[4,32,1024]{2,1,0:T(8,128)(2,1)}, u32[]{:S(2)}) copy-start(bf16[4,32,1024]{2,1,0:T(8,128)(2,1)} %get-tuple-element.49) | copy-start | bytes 786436
  179.8 7.6 %copy-start.25 = (bf16[4,32,1024]{2,1,0:T(8,128)(2,1)S(1)}, bf16[4,32,1024]{2,1,0:T(8,128)(2,1)}, u32[]{:S(2)}) copy-start(bf16[4,32,1024]{2,1,0:T(8,128)(2,1)} %get-tuple-element.50) | copy-start | bytes 786436
  179.8 26.7 %copy-start.24 = (bf16[4,32,1024]{2,1,0:T(8,128)(2,1)S(1)}, bf16[4,32,1024]{2,1,0:T(8,128)(2,1)}, u32[]{:S(2)}) copy-start(bf16[4,32,1024]{2,1,0:T(8,128)(2,1)} %get-tuple-element.51) | copy-start | bytes 786436
  179.8 49.2 %all-to-all-start.6 = ((bf16[4,320,1024]{2,1,0:T(8,128)(2,1)}), bf16[4,320,1024]{2,1,0:T(8,128)(2,1)}, u32[]{:S(2)}, u32[]{:S(2)}) async-start(bf16[4,320,1024]{2,1,0:T(8,128)(2,1)} %get-tuple-element.52), calls=%async_computation.6 | async-start | bytes 5242880 | tf_op jit(solution)/shard_map/all_to_all | solution.py:58
  184.5 22.0 %collective-permute-start.15 = (bf16[4,32,1024]{2,1,0:T(8,128)(2,1)S(1)}, bf16[4,32,1024]{2,1,0:T(8,128)(2,1)S(1)}, u32[]{:S(2)}, u32[]{:S(2)}) collective-permute-start(bf16[4,32,1024]{2,1,0:T(8,128)(2,1)S(1)} %copy-done.26), channel_id=1, source_target_pairs={{0,1},{1,0},{2,3},{3,2},{4,5},{5,4},{6,7},{7,6},{8,9},{9,8},{10,11... | collective-permute-start | bytes 786440 | tf_op jit(solution)/shard_map/ppermute | solution.py:34
  187.4 34.2 %collective-permute-start.16 = (bf16[4,32,1024]{2,1,0:T(8,128)(2,1)S(1)}, bf16[4,32,1024]{2,1,0:T(8,128)(2,1)S(1)}, u32[]{:S(2)}, u32[]{:S(2)}) collective-permute-start(bf16[4,32,1024]{2,1,0:T(8,128)(2,1)S(1)} %copy-done.25), channel_id=1, source_target_pairs={{0,248},{1,249},{2,250},{3,251},{4,252},{5,253},{6,254},{7,255},{8... | collective-permute-start | bytes 786440 | tf_op jit(solution)/shard_map/ppermute | solution.py:34
  206.5 19.7 %collective-permute-start.17 = (bf16[4,32,1024]{2,1,0:T(8,128)(2,1)S(1)}, bf16[4,32,1024]{2,1,0:T(8,128)(2,1)S(1)}, u32[]{:S(2)}, u32[]{:S(2)}) collective-permute-start(bf16[4,32,1024]{2,1,0:T(8,128)(2,1)S(1)} %copy-done.24), channel_id=1, source_target_pairs={{0,249},{1,248},{2,251},{3,250},{4,253},{5,252},{6,255},{7,254},{8... | collective-permute-start | bytes 786440 | tf_op jit(solution)/shard_map/ppermute | solution.py:34
  206.5 19.7 %copy-start.14 = (bf16[4,32,1024]{2,1,0:T(8,128)(2,1)}, bf16[4,32,1024]{2,1,0:T(8,128)(2,1)S(1)}, u32[]{:S(2)}) copy-start(bf16[4,32,1024]{2,1,0:T(8,128)(2,1)S(1)} %collective-permute-done.15.other) | copy-start | bytes 786436
  221.6 4.5 %copy-start.15 = (bf16[4,32,1024]{2,1,0:T(8,128)(2,1)}, bf16[4,32,1024]{2,1,0:T(8,128)(2,1)S(1)}, u32[]{:S(2)}) copy-start(bf16[4,32,1024]{2,1,0:T(8,128)(2,1)S(1)} %collective-permute-done.16.up_own) | copy-start | bytes 786436
  226.1 0.7 copy-start.16
  229.0 12.9 %all-to-all-start.7 = ((bf16[4,64,1024]{2,1,0:T(8,128)(2,1)}), bf16[4,64,1024]{2,1,0:T(8,128)(2,1)S(1)}, u32[]{:S(2)}, u32[]{:S(2)}) async-start(bf16[4,64,1024]{2,1,0:T(8,128)(2,1)} %shard_map.158), calls=%async_computation.7 | async-start | bytes 1048576 | tf_op jit(solution)/shard_map/all_to_all | solution.py:58
  241.9 0.8 copy-start.1
